TPU v7x, 768 devices: a whole 4x8x12 slice. The times are simulated.
768 devices in a mesh: bx: 12 (over z), by: 64 (over x, y, core).
Axes of the slice: x: 4, y: 8, z: 12, core: 2. Of those that a mesh axis runs over, the one named last changes fastest.
Arguments:
- features: float32 [48, 256, 64, 128], P('bx', 'by'), may hold values from -6 to 6
- coords: float32 [48, 256, 3, 128], P('bx', 'by'), as said below
- centers: int32 [12, 64, 32, 128], P('bx', 'by'), may hold values from 0 to 2047, as said below
- neighbours: int32 [12, 64, 32, 128], P('bx', 'by'), may hold values from 0 to 4607, as said below
- live_blocks: int32 [12, 64], P('bx', 'by'), may hold values from 8 to 32, as said below
- w_center: bfloat16 [64, 64], replicated, may hold values from -0.75 to 0.75
- w_neigh: bfloat16 [64, 64], replicated, may hold values from -0.75 to 0.75
- w_radial: float32 [8, 64], replicated, may hold values from -3 to 3
- w_latent: bfloat16 [64, 64], replicated, may hold values from -1 to 1
- w_tensor: bfloat16 [64, 16], replicated, may hold values from -1 to 1
- w_mix: bfloat16 [64, 64], replicated, may hold values from -0.75 to 0.75
- w_env: bfloat16 [16, 64], replicated, may hold values from -3 to 3
- w_out: float32 [64], replicated, may hold values from -1.5 to 1.5
Outputs:
- energies: float32 [48, 256, 128], P('bx', 'by')
- forces: float32 [48, 256, 3, 128], P('bx', 'by')
Inputs may be any that keep to these rules, and one draw needn't show every extreme that they name: `centers`: a center atom of the brick; all edges of one edge block have their center in the same cell; every live edge's center and neighbour lie in the same or adjacent cells and differ in slot by at most 8, never the same atom. `neighbours`: an atom of the extended brick in the center's cell or one of its eight neighbouring cells. `live_blocks`: each brick has either 32 // 4 or 32 live blocks; some brick has 32. `coords`: x and y offsets lie in 0 to 6, z in 0 to 40 and rises with the slot.
All inputs are finite; a program needn't handle non-finite values.
Results may differ from a plain program's by a relative error of at most 0.02.
Values sent between devices are 32-bit elements; how exact they have to be, the bound alone decides.
No kernel may reach another device: no remote copies, remote signals or barrier semaphores. Data moves between devices by JAX's collectives and lax.ppermute only.
A program may use at most 32 MiB of HBM per device.

v0:
```python
import jax
import jax.numpy as jnp
from jax import lax
from jax.sharding import PartitionSpec as P

CELL_WIDTH = 6.0
CUTOFF = 6.0
SOFTEN = 0.25
EXACT = lax.Precision.HIGHEST


def passed_along(array, axis, by):
    length = lax.axis_size(axis)
    return lax.ppermute(array, axis, [(i, (i + by) % length) for i in range(length)])


def extended(cells, sides, width):
    for axis, dim in sides:
        count = lax.axis_size(axis)
        head = lax.slice_in_dim(cells, 0, width, axis=dim)
        tail = lax.slice_in_dim(cells, cells.shape[dim] - width, cells.shape[dim], axis=dim)
        cells = jnp.concatenate(
            [
                lax.ppermute(tail, axis, [(i, (i + 1) % count) for i in range(count)]),
                cells,
                lax.ppermute(head, axis, [((i + 1) % count, i) for i in range(count)]),
            ],
            axis=dim,
        )
    return cells


def edge_terms(
    delta, near_c, near_n, c_hot, own_in, live, w_radial, w_latent, w_tensor, w_mix, w_env, w_out
):
    radius = jnp.sqrt(jnp.sum(delta * delta, 0) + SOFTEN)
    scaled = jnp.minimum(radius / CUTOFF, 1.0)
    envelope = (1.0 - scaled * scaled) ** 2
    orders = jnp.arange(1, w_radial.shape[0] + 1).astype(delta.dtype)
    basis = jnp.sin(orders[:, None] * jnp.pi * scaled[None, :])
    radial = jnp.dot(w_radial.T, basis, precision=EXACT, preferred_element_type=jnp.float32)
    zeta = jax.nn.silu(near_c + near_n + radial).astype(jnp.bfloat16)
    latent = jax.nn.silu(jnp.dot(w_latent.T, zeta, preferred_element_type=jnp.float32)).astype(
        jnp.bfloat16
    )
    chan = jnp.dot(w_tensor.T, latent, preferred_element_type=jnp.float32)
    harm = jnp.concatenate([jnp.ones_like(radius)[None, :], delta / radius[None, :]], 0)
    weight = live * envelope
    spread = (chan[:, None, :] * harm[None, :, :]).reshape(-1, radius.shape[0]) * weight[None, :]
    per_block = spread.reshape(spread.shape[0], c_hot.shape[0], c_hot.shape[1])
    slot_sum = jnp.einsum("kbe,bes->kbs", per_block, c_hot, precision=EXACT)
    gamma = jnp.einsum("kbs,bc->kcs", slot_sum, own_in, precision=EXACT)
    back = jnp.einsum("kcs,bc->kbs", gamma, own_in, precision=EXACT)
    seen = jnp.einsum("kbs,bes->kbe", back, c_hot, precision=EXACT).reshape(chan.shape[0], 4, -1)
    scal = jnp.sum(seen * harm[None, :, :], 1).astype(jnp.bfloat16)
    hidden = jnp.dot(w_mix.T, latent, preferred_element_type=jnp.float32) + jnp.dot(
        w_env.T, scal, preferred_element_type=jnp.float32
    )
    edge_energy = weight * jnp.sum(w_out[:, None] * jax.nn.silu(hidden), 0)
    return (jnp.sum(edge_energy), edge_energy)


def brick(
    feat_ext,
    coord_ext,
    centers,
    neighbours,
    live_count,
    w_center,
    w_neigh,
    w_radial,
    w_latent,
    w_tensor,
    w_mix,
    w_env,
    w_out,
):
    wide_x, wide_y, slots = (feat_ext.shape[0], feat_ext.shape[1], feat_ext.shape[3])
    inner_x, inner_y = (wide_x - 2, wide_y - 2)
    cells_ext = wide_x * wide_y
    cells_in = inner_x * inner_y
    blocks, width = centers.shape
    lat = feat_ext.shape[2]
    table_c = jnp.einsum("lk,xyls->kxys", w_center.astype(jnp.float32), feat_ext, precision=EXACT)
    table_n = jnp.einsum("lk,xyls->kxys", w_neigh.astype(jnp.float32), feat_ext, precision=EXACT)
    anchor_x = jnp.arange(wide_x).astype(coord_ext.dtype) * CELL_WIDTH
    anchor_y = jnp.arange(wide_y).astype(coord_ext.dtype) * CELL_WIDTH
    place_x = coord_ext[:, :, 0, :] + anchor_x[:, None, None]
    place_y = coord_ext[:, :, 1, :] + anchor_y[None, :, None]
    place_z = coord_ext[:, :, 2, :]
    position = jnp.stack([place_x, place_y, place_z])
    source_c = jnp.concatenate([table_c, position], 0).reshape(lat + 3, cells_ext, slots)
    source_n = jnp.concatenate([table_n, position], 0).reshape(lat + 3, cells_ext, slots)
    block_cell = centers[:, 0] // slots
    ext_cell = (block_cell // inner_y + 1) * wide_y + block_cell % inner_y + 1
    offsets = jnp.array(
        [step_x * wide_y + step_y for step_x in (-1, 0, 1) for step_y in (-1, 0, 1)], jnp.int32
    )
    win_cell = ext_cell[:, None] + offsets[None, :]
    ext_iota = jnp.arange(cells_ext, dtype=jnp.int32)
    slot_iota = jnp.arange(slots, dtype=jnp.int32)
    win_map = (win_cell[:, :, None] == ext_iota[None, None, :]).astype(jnp.float32)
    own_ext = (ext_cell[:, None] == ext_iota[None, :]).astype(jnp.float32)
    own_in = (block_cell[:, None] == jnp.arange(cells_in, dtype=jnp.int32)[None, :]).astype(
        jnp.float32
    )
    c_hot = ((centers % slots)[:, :, None] == slot_iota[None, None, :]).astype(jnp.float32)
    n_hot = ((neighbours % slots)[:, :, None] == slot_iota[None, None, :]).astype(jnp.float32)
    n_win = ((neighbours // slots)[:, :, None] == win_cell[:, None, :]).astype(jnp.float32)

    def pick(parts):
        own_row, window, c_row, n_row, w_row = parts
        cell_c = jnp.einsum("rcs,c->rs", source_c, own_row, precision=EXACT)
        got_c = jnp.einsum("rs,es->re", cell_c, c_row, precision=EXACT)
        cell_n = jnp.einsum("rcs,wc->wrs", source_n, window, precision=EXACT)
        slot_n = jnp.einsum("wrs,es->wre", cell_n, n_row, precision=EXACT)
        got_n = jnp.einsum("wre,ew->re", slot_n, w_row, precision=EXACT)
        return (got_c, got_n)

    got_c, got_n = lax.map(pick, (own_ext, win_map, c_hot, n_hot, n_win))
    got_c = jnp.moveaxis(got_c, 0, 1).reshape(lat + 3, -1)
    got_n = jnp.moveaxis(got_n, 0, 1).reshape(lat + 3, -1)
    delta = got_n[lat:] - got_c[lat:]
    near_c = got_c[:lat]
    near_n = got_n[:lat]
    live = (jnp.arange(blocks * width, dtype=jnp.int32) // width < live_count).astype(jnp.float32)

    def energy_of(moved):
        return edge_terms(
            moved,
            near_c,
            near_n,
            c_hot,
            own_in,
            live,
            w_radial,
            w_latent,
            w_tensor,
            w_mix,
            w_env,
            w_out,
        )

    total, pull, edge_energy = jax.vjp(energy_of, delta, has_aux=True)
    grad = pull(jnp.ones_like(total))[0]
    per_slot = jnp.einsum("be,bes->bs", edge_energy.reshape(blocks, width), c_hot, precision=EXACT)
    energies = jnp.einsum("bs,bc->cs", per_slot, own_in, precision=EXACT).reshape(
        inner_x, inner_y, slots
    )
    grad_blocks = grad.reshape(3, blocks, width)
    center_slots = jnp.einsum("kbe,bes->kbs", grad_blocks, c_hot, precision=EXACT)
    push_c = jnp.einsum("kbs,bc->kcs", center_slots, own_ext, precision=EXACT)
    by_window = jnp.einsum("kbe,bew->kbwe", grad_blocks, n_win, precision=EXACT)
    neigh_slots = jnp.einsum("kbwe,bes->kbws", by_window, n_hot, precision=EXACT)
    push_n = jnp.einsum("kbws,bwc->kcs", neigh_slots, win_map, precision=EXACT)
    push = (push_c - push_n).reshape(3, wide_x, wide_y, slots)
    push = jnp.moveaxis(push, 0, 2)
    return (energies, push)


def return_along_x(pushed):
    inner = pushed.shape[0] - 2
    for direction, source, target in ((-1, 0, inner), (1, inner + 1, 1)):
        arrived = passed_along(pushed[source], "bx", direction)
        pushed = pushed.at[target].add(arrived)
    return pushed[1 : inner + 1]


def return_along_y(pushed):
    inner = pushed.shape[1] - 2
    for direction, source, target in ((-1, 0, inner), (1, inner + 1, 1)):
        arrived = passed_along(pushed[:, source], "by", direction)
        pushed = pushed.at[:, target].add(arrived)
    return pushed[:, 1 : inner + 1]


def body(
    features,
    coords,
    centers,
    neighbours,
    live_blocks,
    w_center,
    w_neigh,
    w_radial,
    w_latent,
    w_tensor,
    w_mix,
    w_env,
    w_out,
):
    feat_ext, coord_ext = (
        extended(features, (("bx", 0), ("by", 1)), 1),
        extended(coords, (("bx", 0), ("by", 1)), 1),
    )
    live_count = live_blocks[0, 0]
    center_list = centers[0, 0]
    neigh_list = neighbours[0, 0]
    weights = (w_center, w_neigh, w_radial, w_latent, w_tensor, w_mix, w_env, w_out)
    energies, pushed = brick(feat_ext, coord_ext, center_list, neigh_list, live_count, *weights)
    forces = return_along_y(return_along_x(pushed))
    return (energies, forces)


def solution(mesh):
    placed = (
        P("bx", "by", None, None),
        P("bx", "by", None, None),
        P("bx", "by", None, None),
        P("bx", "by", None, None),
        P("bx", "by"),
        P(),
        P(),
        P(),
        P(),
        P(),
        P(),
        P(),
        P(),
    )
    return jax.shard_map(
        body,
        mesh=mesh,
        in_specs=placed,
        out_specs=(P("bx", "by", None), P("bx", "by", None, None)),
        check_vma=False,
    )
```

profile of v0, /device:TPU:1, one launch (start us, length us, event | category | flops | bytes accessed | tf_op | source)
XLA Modules:
  0.0 304.0 jit_solution(10117072404579498023)
XLA Ops:
  1.6 4.8 %collective-permute-start = (f32[1,4,64,128]{3,2,1,0:T(8,128)S(1)}, f32[1,4,64,128]{3,2,1,0:T(8,128)S(1)}, u32[]{:S(2)}, u32[]{:S(2)}) collective-permute-start(f32[1,4,64,128]{3,2,1,0:T(8,128)S(1)} %get-tuple-element.138), channel_id=1, source_target_pairs={{0,64},{64,128},{128,192},{192,256},{256,320},{320,384},{384,448},... | collective-permute-start | bytes 393224 | tf_op jit(solution)/shard_map/ppermute | solution.py:24
  6.5 12.2 %collective-permute-start.1 = (f32[1,4,64,128]{3,2,1,0:T(8,128)S(1)}, f32[1,4,64,128]{3,2,1,0:T(8,128)S(1)}, u32[]{:S(2)}, u32[]{:S(2)}) collective-permute-start(f32[1,4,64,128]{3,2,1,0:T(8,128)S(1)} %get-tuple-element.137), channel_id=1, source_target_pairs={{64,0},{128,64},{192,128},{256,192},{320,256},{384,320},{448,384},... | collective-permute-start | bytes 393224 | tf_op jit(solution)/shard_map/ppermute | solution.py:26
  19.4 1.9 collective-permute-start.4
  21.3 4.6 %collective-permute-start.5 = (f32[1,4,3,128]{3,1,2,0:T(4,128)S(1)}, f32[1,4,3,128]{3,1,2,0:T(4,128)S(1)}, u32[]{:S(2)}, u32[]{:S(2)}) collective-permute-start(f32[1,4,3,128]{3,1,2,0:T(4,128)S(1)} %get-tuple-element.150), channel_id=1, source_target_pairs={{64,0},{128,64},{192,128},{256,192},{320,256},{384,320},{448,384},... | collective-permute-start | bytes 18440 | tf_op jit(solution)/shard_map/ppermute | solution.py:26
  30.5 3.1 %fusion.31 = (f32[32,128,128]{2,1,0:T(8,128)}, f32[32,128,128]{2,1,0:T(8,128)}) fusion(s32[32,128]{1,0:T(8,128)S(1)} %get-tuple-element.159, s32[32,128]{1,0:T(8,128)S(1)} %add_select_fusion.4), kind=kLoop, calls=%fused_computation.45 | loop fusion | flops 2097152 | bytes 4227072 | tf_op jit(solution)/shard_map/convert_element_type | solution.py:108
  33.6 4.7 %collective-permute-start.6 = (f32[6,1,3,128]{3,1,2,0:T(1,128)S(1)}, f32[6,1,3,128]{3,1,2,0:T(1,128)S(1)}, u32[]{:S(2)}, u32[]{:S(2)}) collective-permute-start(f32[6,1,3,128]{3,1,2,0:T(1,128)S(1)} %get-tuple-element.148), channel_id=1, source_target_pairs={{0,1},{1,2},{2,3},{3,4},{4,5},{5,6},{6,7},{7,8},{8,9},{9,10},{10,1... | collective-permute-start | bytes 27656 | tf_op jit(solution)/shard_map/ppermute | solution.py:24
  38.4 1.9 collective-permute-start.7
  43.8 2.2 collective-permute-start.2
  46.0 4.1 %collective-permute-start.3 = (f32[6,1,64,128]{3,2,1,0:T(8,128)S(1)}, f32[6,1,64,128]{3,2,1,0:T(8,128)S(1)}, u32[]{:S(2)}, u32[]{:S(2)}) collective-permute-start(f32[6,1,64,128]{3,2,1,0:T(8,128)S(1)} %get-tuple-element.136), channel_id=1, source_target_pairs={{1,0},{2,1},{3,2},{4,3},{5,4},{6,5},{7,6},{8,7},{9,8},{10,9},{11,1... | collective-permute-start | bytes 589832 | tf_op jit(solution)/shard_map/ppermute | solution.py:26
  50.2 2.8 collective-permute-done.3
  56.1 175.2 %while.16 = (s32[]{:T(128)}, f32[32,67,128]{2,1,0:T(8,128)}, f32[32,67,128]{2,1,0:T(8,128)}, f32[32,36]{1,0:T(8,128)S(1)}, f32[67,36,128]{2,1,0:T(8,128)S(1)}, /...) while((s32[]{:T(128)}, f32[32,67,128]{2,1,0:T(8,128)}, ...), condition=%wide.region_1.2_spmd, body=%wide.region_0.1_spmd.sunk | while | flops 168921472 | bytes 3728505 | solution.py:120
  59.9 1.7 fusion.209
  70.8 1.7 fusion.209
  81.8 1.7 fusion.209
  92.7 1.7 fusion.209
  98.2 1.7 fusion.209
  103.6 1.7 fusion.209
  109.1 1.7 fusion.209
  125.5 1.7 fusion.209
  136.5 1.7 fusion.209
  142.0 1.7 fusion.209
  147.4 1.7 fusion.209
  152.9 1.7 fusion.209
  158.4 1.7 fusion.209
  169.3 1.7 fusion.209
  174.8 1.7 fusion.209
  180.3 1.7 fusion.209
  185.7 1.7 fusion.209
  191.2 1.7 fusion.209
  196.7 1.7 fusion.209
  207.6 1.7 fusion.209
  218.6 1.7 fusion.209
  224.1 1.7 fusion.209
  233.1 3.0 fusion.20
  239.8 2.3 fusion.41
  243.8 3.1 %fusion.42 = f32[64,32,128]{2,0,1:T(8,128)S(1)} fusion(f32[64,32,128]{2,1,0:T(8,128)S(1)} %convolution_bitcast_fusion.7, s32[32,128]{1,0:T(8,128)S(1)} %add_select_fusion.4), kind=kOutput, calls=%fused_computation.67 | convolution fusion | flops 403177472 | bytes 2113536 | tf_op jit(solution)/shard_map/jvp(kbs,bes->kbe)/dot_general | solution.py:54
  254.5 3.1 %fusion.34 = f32[32,64,128]{2,1,0:T(8,128)S(1)} fusion(f32[64,32,128]{2,1,0:T(8,128)S(1)} %mul.295, s32[32,128]{1,0:T(8,128)} %copy-done.6), kind=kOutput, calls=%fused_computation.49 | convolution fusion | flops 403177472 | bytes 2113536 | tf_op jit(solution)/shard_map/transpose(jvp(kbs,bes->kbe))/dot_general | solution.py:54
  259.3 3.4 %fusion.60 = (f32[32,128]{1,0:T(8,128)S(1)}, f32[64,32,128]{2,0,1:T(8,128)S(1)}) fusion(f32[64,32,128]{2,1,0:T(8,128)S(1)} %mul.278, s32[32,128]{1,0:T(8,128)S(1)} %copy-done.7, f32[32,128,64]{1,0,2:T(8,128)S(1)} %convolution_bitcast_fusion.6), kind=kOutput, calls=%fused_computation.89 | convolution fusion | flops 403697664 | bytes 3178496 | tf_op jit(solution)/shard_map/transpose(jvp(kbe,bes->kbs))/dot_general | solution.py:51
  265.4 3.7 %fusion.22 = f32[64,4096]{1,0:T(8,128)} fusion(bf16[64,64]{1,0:T(8,128)(2,1)S(1)} %copy-done, f32[64,4096]{1,0:T(8,128)} %get-tuple-element.162, bf16[4096,64]{0,1:T(8,128)(2,1)S(1)} %fusion.166, bf16[64,64]{1,0:T(8,128)(2,1)S(1)} %copy-done.28, f32[64,4096]{1,0:T(8,128)} %copy-done.40, f32[4096]{0:T(1024)S(1)} %copy-done.20, f32[64]{0:T(128)S(1)} %copy-done.39), kind=kOutput, calls=%fused_computation.30 | convolution fusion | flops 73400320 | bytes 3703040 | tf_op jit(solution)/shard_map/transpose(jvp())/dot_general | solution.py:43
  269.2 2.6 fusion.47
  273.8 2.0 fusion.44
  276.6 2.4 collective-permute-start.8
  279.1 2.0 collective-permute-done.8
  281.1 1.9 collective-permute-start.9
  283.1 3.7 %collective-permute-done.9 = f32[6,3,128]{2,1,0:T(4,128)S(1)} collective-permute-done((f32[6,3,128]{2,1,0:T(4,128)S(1)}, f32[6,3,128]{2,1,0:T(4,128)S(1)}, u32[]{:S(2)}, u32[]{:S(2)}) %collective-permute-start.9) | collective-permute-done | bytes 9248 | tf_op jit(solution)/shard_map/ppermute | solution.py:14
  286.8 9.5 %collective-permute-start.10 = (f32[4,3,128]{2,0,1:T(4,128)S(1)}, f32[4,3,128]{2,0,1:T(4,128)S(1)}, u32[]{:S(2)}, u32[]{:S(2)}) collective-permute-start(f32[4,3,128]{2,0,1:T(4,128)S(1)} %slice_bitcast_fusion.4), channel_id=1, source_target_pairs={{0,63},{1,0},{2,1},{3,2},{4,3},{5,4},{6,5},{7,6},{8,7},{9,8},{10,9... | collective-permute-start | bytes 18440 | tf_op jit(solution)/shard_map/ppermute | solution.py:14
  297.9 1.9 collective-permute-start.11
  300.5 2.8 collective-permute-done.11
  (352 shorter events, 173.1 us)
Async XLA Ops:
  0.6 235.4 %copy-start = (bf16[64,64]{1,0:T(8,128)(2,1)S(1)}, bf16[64,64]{1,0:T(8,128)(2,1)}, u32[]{:S(2)}) copy-start(bf16[64,64]{1,0:T(8,128)(2,1)} %param.32) | copy-start | bytes 24580
  1.6 42.0 %collective-permute-start = (f32[1,4,64,128]{3,2,1,0:T(8,128)S(1)}, f32[1,4,64,128]{3,2,1,0:T(8,128)S(1)}, u32[]{:S(2)}, u32[]{:S(2)}) collective-permute-start(f32[1,4,64,128]{3,2,1,0:T(8,128)S(1)} %get-tuple-element.138), channel_id=1, source_target_pairs={{0,64},{64,128},{128,192},{192,256},{256,320},{320,384},{384,448},... | collective-permute-start | bytes 393224 | tf_op jit(solution)/shard_map/ppermute | solution.py:24
  6.5 37.2 %collective-permute-start.1 = (f32[1,4,64,128]{3,2,1,0:T(8,128)S(1)}, f32[1,4,64,128]{3,2,1,0:T(8,128)S(1)}, u32[]{:S(2)}, u32[]{:S(2)}) collective-permute-start(f32[1,4,64,128]{3,2,1,0:T(8,128)S(1)} %get-tuple-element.137), channel_id=1, source_target_pairs={{64,0},{128,64},{192,128},{256,192},{320,256},{384,320},{448,384},... | collective-permute-start | bytes 393224 | tf_op jit(solution)/shard_map/ppermute | solution.py:26
  19.4 14.1 %collective-permute-start.4 = (f32[1,4,3,128]{3,1,2,0:T(4,128)S(1)}, f32[1,4,3,128]{3,1,2,0:T(4,128)S(1)}, u32[]{:S(2)}, u32[]{:S(2)}) collective-permute-start(f32[1,4,3,128]{3,1,2,0:T(4,128)S(1)} %get-tuple-element.151), channel_id=1, source_target_pairs={{0,64},{64,128},{128,192},{192,256},{256,320},{320,384},{384,448},... | collective-permute-start | bytes 18440 | tf_op jit(solution)/shard_map/ppermute | solution.py:24
  21.3 12.3 %collective-permute-start.5 = (f32[1,4,3,128]{3,1,2,0:T(4,128)S(1)}, f32[1,4,3,128]{3,1,2,0:T(4,128)S(1)}, u32[]{:S(2)}, u32[]{:S(2)}) collective-permute-start(f32[1,4,3,128]{3,1,2,0:T(4,128)S(1)} %get-tuple-element.150), channel_id=1, source_target_pairs={{64,0},{128,64},{192,128},{256,192},{320,256},{384,320},{448,384},... | collective-permute-start | bytes 18440 | tf_op jit(solution)/shard_map/ppermute | solution.py:26
  26.7 217.1 %copy-start.6 = (s32[32,128]{1,0:T(8,128)}, s32[32,128]{1,0:T(8,128)S(1)}, u32[]{:S(2)}) copy-start(s32[32,128]{1,0:T(8,128)S(1)} %add_select_fusion.4) | copy-start | bytes 49156
  27.4 3.1 %copy-start.13 = (s32[32,128]{1,0:T(8,128)}, s32[32,128]{1,0:T(8,128)S(1)}, u32[]{:S(2)}) copy-start(s32[32,128]{1,0:T(8,128)S(1)} %get-tuple-element.159) | copy-start | bytes 49156
  28.3 214.9 %copy-start.24 = (s32[32]{0:T(128)}, s32[32]{0:T(128)S(1)}, u32[]{:S(2)}) copy-start(s32[32]{0:T(128)S(1)} %get-tuple-element.111) | copy-start | bytes 388
  30.5 3.1 %copy-start.23 = (f32[4,4,3,128]{3,1,2,0:T(4,128)S(1)}, f32[4,4,3,128]{3,1,2,0:T(4,128)}, u32[]{:S(2)}) copy-start(f32[4,4,3,128]{3,1,2,0:T(4,128)} %param.25) | copy-start | bytes 73732
  33.6 10.1 %copy-start.3 = (f32[4,4,64,128]{3,2,1,0:T(8,128)S(1)}, f32[4,4,64,128]{3,2,1,0:T(8,128)}, u32[]{:S(2)}) copy-start(f32[4,4,64,128]{3,2,1,0:T(8,128)} %param.24) | copy-start | bytes 1572868
  33.6 8.3 %collective-permute-start.6 = (f32[6,1,3,128]{3,1,2,0:T(1,128)S(1)}, f32[6,1,3,128]{3,1,2,0:T(1,128)S(1)}, u32[]{:S(2)}, u32[]{:S(2)}) collective-permute-start(f32[6,1,3,128]{3,1,2,0:T(1,128)S(1)} %get-tuple-element.148), channel_id=1, source_target_pairs={{0,1},{1,2},{2,3},{3,4},{4,5},{5,6},{6,7},{7,8},{8,9},{9,10},{10,1... | collective-permute-start | bytes 27656 | tf_op jit(solution)/shard_map/ppermute | solution.py:24
  38.4 5.0 %collective-permute-start.7 = (f32[6,1,3,128]{3,1,2,0:T(1,128)S(1)}, f32[6,1,3,128]{3,1,2,0:T(1,128)S(1)}, u32[]{:S(2)}, u32[]{:S(2)}) collective-permute-start(f32[6,1,3,128]{3,1,2,0:T(1,128)S(1)} %get-tuple-element.149), channel_id=1, source_target_pairs={{1,0},{2,1},{3,2},{4,3},{5,4},{6,5},{7,6},{8,7},{9,8},{10,9},{11,1... | collective-permute-start | bytes 27656 | tf_op jit(solution)/shard_map/ppermute | solution.py:26
  40.3 192.7 %copy-start.35 = (f32[8]{0:T(128)}, f32[8]{0:T(128)S(1)}, u32[]{:S(2)}) copy-start(f32[8]{0:T(128)S(1)} %convert_multiply_fusion) | copy-start | bytes 100
  43.4 9.6 %copy-start.26 = (bf16[64,64]{1,0:T(8,128)(2,1)S(1)}, bf16[64,64]{1,0:T(8,128)(2,1)}, u32[]{:S(2)}) copy-start(bf16[64,64]{1,0:T(8,128)(2,1)} %param.29) | copy-start | bytes 24580
  43.8 6.4 %collective-permute-start.2 = (f32[6,1,64,128]{3,2,1,0:T(8,128)S(1)}, f32[6,1,64,128]{3,2,1,0:T(8,128)S(1)}, u32[]{:S(2)}, u32[]{:S(2)}) collective-permute-start(f32[6,1,64,128]{3,2,1,0:T(8,128)S(1)} %get-tuple-element.135), channel_id=1, source_target_pairs={{0,1},{1,2},{2,3},{3,4},{4,5},{5,6},{6,7},{7,8},{8,9},{9,10},{10,1... | collective-permute-start | bytes 589832 | tf_op jit(solution)/shard_map/ppermute | solution.py:24
  46.0 7.0 %collective-permute-start.3 = (f32[6,1,64,128]{3,2,1,0:T(8,128)S(1)}, f32[6,1,64,128]{3,2,1,0:T(8,128)S(1)}, u32[]{:S(2)}, u32[]{:S(2)}) collective-permute-start(f32[6,1,64,128]{3,2,1,0:T(8,128)S(1)} %get-tuple-element.136), channel_id=1, source_target_pairs={{1,0},{2,1},{3,2},{4,3},{5,4},{6,5},{7,6},{8,7},{9,8},{10,9},{11,1... | collective-permute-start | bytes 589832 | tf_op jit(solution)/shard_map/ppermute | solution.py:26
  56.1 177.0 %copy-start.33 = (f32[8,64]{1,0:T(8,128)S(1)}, f32[8,64]{1,0:T(8,128)}, u32[]{:S(2)}) copy-start(f32[8,64]{1,0:T(8,128)} %param.31) | copy-start | bytes 6148
  233.0 3.1 %copy-start.17 = (f32[4096]{0:T(1024)}, f32[4096]{0:T(1024)S(1)}, u32[]{:S(2)}) copy-start(f32[4096]{0:T(1024)S(1)} %get-tuple-element.155) | copy-start | bytes 49156
  236.1 1.6 copy-start.4
  236.1 2.4 copy-start.29
  237.6 0.8 copy-start.1
  247.9 1.0 copy-start.2
  247.9 2.1 copy-start.37
  247.9 2.1 copy-start.38
  250.0 2.2 copy-start.19
  251.2 1.0 copy-start.40
  254.5 3.1 %copy-start.25 = (s32[32]{0:T(128)S(1)}, s32[32]{0:T(128)}, u32[]{:S(2)}) copy-start(s32[32]{0:T(128)} %copy-done.24) | copy-start | bytes 388
  257.6 1.7 copy-start.7
  263.4 1.6 copy-start.30
  264.1 1.3 copy-start.28
  264.1 1.3 copy-start.39
  265.4 3.8 %copy-start.5 = (f32[64,4096]{1,0:T(8,128)S(1)}, f32[64,4096]{1,0:T(8,128)}, u32[]{:S(2)}) copy-start(f32[64,4096]{1,0:T(8,128)} %copy-done.4) | copy-start | bytes 3145732
  265.4 3.8 %copy-start.18 = (f32[4096]{0:T(1024)S(1)}, f32[4096]{0:T(1024)}, u32[]{:S(2)}) copy-start(f32[4096]{0:T(1024)} %copy-done.17) | copy-start | bytes 49156
  265.4 3.8 %copy-start.34 = (f32[8,64]{1,0:T(8,128)S(1)}, f32[8,64]{1,0:T(8,128)}, u32[]{:S(2)}) copy-start(f32[8,64]{1,0:T(8,128)} %param.31) | copy-start | bytes 6148
  265.4 3.8 %copy-start.36 = (f32[8]{0:T(128)S(1)}, f32[8]{0:T(128)}, u32[]{:S(2)}) copy-start(f32[8]{0:T(128)} %copy-done.35) | copy-start | bytes 100
  269.1 2.7 copy-start.9
  269.2 2.7 copy-start.21
  269.2 2.8 copy-start.11
  269.2 2.8 copy-start.22
  269.2 2.8 copy-start.16
  271.8 2.0 copy-start.8
  271.8 2.0 copy-start.14
  273.7 2.1 copy-start.12
  273.8 2.5 copy-start.32
  276.6 4.4 %collective-permute-start.8 = (f32[6,3,128]{2,1,0:T(4,128)S(1)}, f32[6,3,128]{2,1,0:T(4,128)S(1)}, u32[]{:S(2)}, u32[]{:S(2)}) collective-permute-start(f32[6,3,128]{2,1,0:T(4,128)S(1)} %slice_bitcast_fusion.1), channel_id=1, source_target_pairs={{0,704},{64,0},{128,64},{192,128},{256,192},{320,256},{384,320},{4... | collective-permute-start | bytes 27656 | tf_op jit(solution)/shard_map/ppermute | solution.py:14
  281.1 5.7 %collective-permute-start.9 = (f32[6,3,128]{2,1,0:T(4,128)S(1)}, f32[6,3,128]{2,1,0:T(4,128)S(1)}, u32[]{:S(2)}, u32[]{:S(2)}) collective-permute-start(f32[6,3,128]{2,1,0:T(4,128)S(1)} %get-tuple-element.141), channel_id=1, source_target_pairs={{0,64},{64,128},{128,192},{192,256},{256,320},{320,384},{384,448},... | collective-permute-start | bytes 27656 | tf_op jit(solution)/shard_map/ppermute | solution.py:14
  286.8 11.0 %collective-permute-start.10 = (f32[4,3,128]{2,0,1:T(4,128)S(1)}, f32[4,3,128]{2,0,1:T(4,128)S(1)}, u32[]{:S(2)}, u32[]{:S(2)}) collective-permute-start(f32[4,3,128]{2,0,1:T(4,128)S(1)} %slice_bitcast_fusion.4), channel_id=1, source_target_pairs={{0,63},{1,0},{2,1},{3,2},{4,3},{5,4},{6,5},{7,6},{8,7},{9,8},{10,9... | collective-permute-start | bytes 18440 | tf_op jit(solution)/shard_map/ppermute | solution.py:14
  297.9 5.5 %collective-permute-start.11 = (f32[4,3,128]{2,0,1:T(4,128)S(1)}, f32[4,3,128]{2,0,1:T(4,128)S(1)}, u32[]{:S(2)}, u32[]{:S(2)}) collective-permute-start(f32[4,3,128]{2,0,1:T(4,128)S(1)} %slice_bitcast_fusion.3), channel_id=1, source_target_pairs={{0,1},{1,2},{2,3},{3,4},{4,5},{5,6},{6,7},{7,8},{8,9},{9,10},{10,1... | collective-permute-start | bytes 18440 | tf_op jit(solution)/shard_map/ppermute | solution.py:14
  (5 other events, 3.4 us)
where the time goes:
time: 309 us; the launch traced here: 304 us
  matrix products  192 us (62%)
  starting transfers between devices  52.3 us (17%)
  local copies, waits for them, and re-layouts  31.6 us (10%)
  waiting for transfers between devices  12.7 us (4%)
  other arithmetic  12.5 us (4%)
    dot_general x32, matrix products, pick(): got_c = jnp.einsum('rs,es->re', cell_c, c_row, precision=EXACT)  55.2 us
    dot_general x32, matrix products, pick(): slot_n = jnp.einsum('wrs,es->wre', cell_n, n_row, precision=EXACT)  49.1 us
    dot_general x32, matrix products, pick(): cell_n = jnp.einsum('rcs,wc->wrs', source_n, window, precision=EXACT)  25.5 us
    dot_general x32, matrix products, pick(): cell_c = jnp.einsum('rcs,c->rs', source_c, own_row, precision=EXACT)  24.4 us
    ppermute x4, starting transfers between devices, extended(): lax.ppermute(head, axis, [((i + 1) % count, i) for i in range(count)])  22.8 us
    dynamic_update_slice x32, local copies, waits for them, and re-layouts, brick(): got_c, got_n = lax.map(pick, (own_ext, win_map, c_hot, n_hot, n_win))  19.8 us
    ppermute x4, starting transfers between devices, passed_along(): lax.ppermute(array, axis, [(i, (i + by) % length) for i in range(length)])  15.8 us
    ppermute x4, starting transfers between devices, extended(): lax.ppermute(tail, axis, [(i, (i + 1) % count) for i in range(count)])  13.7 us
  transfers between devices with their start and end apart: 12, of which 5 were waited for; matrix products, arithmetic and copies ran while one was open for 4% of the time, Pallas kernels for 0%

commit v1 on v0

v1 whole, which is shorter than its diff:
```python
import jax
import jax.numpy as jnp
from jax import lax
from jax.experimental import pallas as pl
from jax.experimental.pallas import tpu as pltpu
from jax.sharding import PartitionSpec as P

CELL_WIDTH = 6.0
CUTOFF = 6.0
SOFTEN = 0.25
ROWS = 72
GROUP = 8
F32 = jnp.float32
BF16 = jnp.bfloat16
SIN_TERMS = (3.14159265358979, -5.16771278004997, 2.55016403987735, -0.599264529320792, 0.0821458866111282, -0.00737043094571435)
COS_TERMS = (1.0, -4.93480220054468, 4.05871212641677, -1.33526276885459, 0.235330630358893, -0.0258068913900141, 0.00192957430940392)


def shifted(array, axis, by):
    length = lax.axis_size(axis)
    return lax.ppermute(array, axis, [(i, (i + by) % length) for i in range(length)])


def split(array):
    high = array.astype(BF16).astype(F32)
    return high, array - high


def dot_tn(left, right):
    return lax.dot_general(left, right, (((0,), (0,)), ((), ())), preferred_element_type=F32)


def dot_nt(left, right):
    return lax.dot_general(left, right, (((1,), (1,)), ((), ())), preferred_element_type=F32)


def dot_nn(left, right):
    return jnp.dot(left, right, preferred_element_type=F32)


def tables_kernel(feat, coord, w_center, w_neigh, table_c, packed):
    inner_x, inner_y, lat, slots = feat.shape
    both = jnp.concatenate([w_center[...].astype(F32), w_neigh[...].astype(F32)], 1)
    both = jnp.concatenate([both, both], 0).T.astype(BF16)
    pad = jnp.zeros((ROWS - lat - 3, slots), F32)
    for x in range(inner_x):
        flat = jnp.concatenate([feat[x, y] for y in range(inner_y)], 1)
        high, low = split(flat)
        out = dot_nn(both, jnp.concatenate([high, low], 0).astype(BF16))
        for y in range(inner_y):
            piece = out[:, y * slots : (y + 1) * slots]
            table_c[x * inner_y + y] = piece[:lat]
            packed[x, y, :lat] = piece[lat:]
            packed[x, y, lat:] = jnp.concatenate([coord[x, y], pad], 0)


def tables(features, coords, w_center, w_neigh):
    inner_x, inner_y, lat, slots = features.shape
    return pl.pallas_call(
        tables_kernel,
        out_shape=(
            jax.ShapeDtypeStruct((inner_x * inner_y, lat, slots), F32),
            jax.ShapeDtypeStruct((inner_x, inner_y, ROWS, slots), F32),
        ),
        compiler_params=pltpu.CompilerParams(vmem_limit_bytes=16 * 1024 * 1024),
    )(features, coords, w_center, w_neigh)


def sine_cosine(turns):
    whole = jnp.floor(turns + 0.5)
    part = turns - whole
    sign = 1.0 - 2.0 * (whole - 2.0 * jnp.floor(0.5 * whole))
    square = part * part

    def poly(terms):
        total = jnp.full_like(square, terms[-1])
        for term in terms[-2::-1]:
            total = total * square + term
        return total

    return sign * part * poly(SIN_TERMS), sign * poly(COS_TERMS)


def gated(value):
    gate = 0.5 * jnp.tanh(0.5 * value) + 0.5
    silu = value * gate
    return silu, gate + silu - silu * gate


def brick_kernel(
    cells,
    live,
    centers,
    neighbours,
    table_c,
    packed,
    west,
    east,
    south,
    north,
    w_radial,
    w_latent,
    w_tensor,
    w_mix,
    w_env,
    w_out,
    energies,
    push_west,
    push_east,
    push_inner,
    table_n,
    gamma,
    g_gamma,
    push,
    slope_z,
    slope_l,
    latent_s,
    g_hidden_s,
    chan_s,
    rows_s,
    sems,
):
    inner_x, inner_y, _, slots = packed.shape
    wide_y = inner_y + 2
    lat = w_latent.shape[0]
    ch = w_tensor.shape[1]
    nb = w_radial.shape[0]
    width = GROUP * slots
    copies = []
    for x in range(inner_x):
        copies.append((packed.at[x], (x + 1) * wide_y + 1, inner_y))
    copies.append((west.at[0], 1, inner_y))
    copies.append((east.at[0], (inner_x + 1) * wide_y + 1, inner_y))
    for x in range(inner_x + 2):
        copies.append((south.at[x], x * wide_y, 1))
        copies.append((north.at[x], x * wide_y + inner_y + 1, 1))
    started = []
    for i, (source, at, count) in enumerate(copies):
        copy = pltpu.make_async_copy(source, table_n.at[pl.ds(at, count)], sems.at[i])
        copy.start()
        started.append(copy)

    gamma[...] = jnp.zeros_like(gamma)
    g_gamma[...] = jnp.zeros_like(g_gamma)
    push[...] = jnp.zeros_like(push)
    wr_high, wr_low = split(w_radial[...])
    wr_fwd = jnp.concatenate([wr_high, wr_high, wr_low, wr_low], 0).astype(BF16)
    wr_bwd = jnp.concatenate([wr_high, wr_low], 0).astype(BF16)
    orders = lax.broadcasted_iota(jnp.int32, (nb, 1), 0).astype(F32) + 1.0
    slot_iota = lax.broadcasted_iota(jnp.int32, (slots, slots), 0)
    row_iota = lax.broadcasted_iota(jnp.int32, (8, 1), 0)
    force_rows = jnp.where((row_iota & 3) == 3, 0.0, 1.0)
    out_col = w_out[...]
    offsets = [dx * wide_y + dy for dx in (-1, 0, 1) for dy in (-1, 0, 1)]
    groups = live[0, 0] // GROUP
    for copy in started:
        copy.wait()

    def cell_of(block):
        cell = cells[0, 0, block, 0] // slots
        cell_x = cell // inner_y
        return cell, (cell_x + 1) * wide_y + (cell - cell_x * inner_y) + 1

    def hot(slot):
        return jnp.where(slot_iota == slot, 1.0, 0.0).astype(BF16)

    def lanes(array, j):
        return array[:, j * slots : (j + 1) * slots]

    def gathered(table, slot_rows, blocks):
        parts = []
        for j in range(GROUP):
            cell, _ = cell_of(blocks + j)
            index = jnp.broadcast_to(slot_rows[j : j + 1], (4 * ch, slots))
            parts.append(jnp.take_along_axis(table[cell], index, axis=1))
        return jnp.concatenate(parts, 1)

    def scattered(table, values, slot_rows, blocks):
        for j in range(GROUP):
            cell, _ = cell_of(blocks + j)
            out = dot_nt(lanes(values, j).astype(BF16), hot(slot_rows[j : j + 1]))
            rows = table.shape[1]
            table[cell] += sum(out[i : i + rows] for i in range(0, out.shape[0], rows))

    def forward(g, carry):
        blocks = pl.multiple_of(g * GROUP, GROUP)
        c_rows = centers[0, 0, pl.ds(blocks, GROUP), :] & (slots - 1)
        n_all = neighbours[0, 0, pl.ds(blocks, GROUP), :]
        n_rows = n_all & (slots - 1)
        n_cells = n_all >> 7
        n_x = (n_cells * 43) >> 8
        n_y = n_cells - n_x * wide_y
        near_parts, delta_parts = [], []
        for j in range(GROUP):
            cell, ext = cell_of(blocks + j)
            ext_x = cell // inner_y + 1
            ext_y = cell - (ext_x - 1) * inner_y + 1
            c_index = jnp.broadcast_to(c_rows[j : j + 1], (lat, slots))
            n_index = jnp.broadcast_to(n_rows[j : j + 1], (ROWS, slots))
            n_cell = jnp.broadcast_to(n_cells[j : j + 1] - ext, (ROWS, slots))
            near_c = jnp.take_along_axis(table_c[cell], c_index, axis=1)
            place_c = jnp.take_along_axis(table_n[ext, lat:], c_index[:8], axis=1)
            got = jnp.zeros((ROWS, slots), F32)
            for offset in offsets:
                piece = jnp.take_along_axis(table_n[ext + offset], n_index, axis=1)
                got = jnp.where(n_cell == offset, piece, got)
            near_parts.append(near_c + got[:lat])
            step_x = (n_x[j : j + 1] - ext_x).astype(F32) * CELL_WIDTH
            step_y = (n_y[j : j + 1] - ext_y).astype(F32) * CELL_WIDTH
            step = jnp.where(row_iota == 0, step_x, jnp.where(row_iota == 1, step_y, 0.0))
            delta_parts.append(got[lat:] - place_c + step)
        near = jnp.concatenate(near_parts, 1)
        delta = jnp.concatenate(delta_parts, 1)
        square = delta * delta
        length2 = square[0:1] + square[1:2] + square[2:3] + SOFTEN
        inverse = lax.rsqrt(length2)
        scaled = jnp.minimum(length2 * inverse * (1.0 / CUTOFF), 1.0)
        fall = 1.0 - scaled * scaled
        weight = fall * fall
        harm = delta * inverse
        basis, _ = sine_cosine(orders * scaled)
        b_high, b_low = split(basis)
        b_all = jnp.concatenate([b_high, b_low, b_high, b_low], 0).astype(BF16)
        zeta, slope = gated(near + dot_tn(wr_fwd, b_all))
        slope_z[g] = slope
        latent, slope = gated(dot_tn(w_latent[...], zeta.astype(BF16)))
        slope_l[g] = slope
        latent = latent.astype(BF16)
        latent_s[g] = latent
        chan = dot_tn(w_tensor[...], latent)
        chan_s[g] = chan
        rows_s[g, 0:3] = harm[0:3]
        rows_s[g, 3:4] = weight
        rows_s[g, 4:5] = scaled
        rows_s[g, 5:6] = inverse
        heavy = chan * weight
        spread = jnp.concatenate([heavy] + [heavy * harm[m : m + 1] for m in range(3)], 0)
        scattered(gamma, jnp.concatenate(split(spread), 0), c_rows, blocks)
        return carry

    lax.fori_loop(0, groups, forward, 0)

    def middle(g, carry):
        blocks = pl.multiple_of(g * GROUP, GROUP)
        c_rows = centers[0, 0, pl.ds(blocks, GROUP), :] & (slots - 1)
        seen = gathered(gamma, c_rows, blocks)
        weight = rows_s[g, 3:4]
        harm = [rows_s[g, m : m + 1] for m in range(3)]
        scal = seen[:ch]
        for m in range(3):
            scal = scal + harm[m] * seen[(m + 1) * ch : (m + 2) * ch]
        hidden = dot_tn(w_mix[...], latent_s[g]) + dot_tn(w_env[...], scal.astype(BF16))
        lifted, slope = gated(hidden)
        value = jnp.sum(out_col * lifted, 0, keepdims=True)
        g_hidden = ((out_col * slope) * weight).astype(BF16)
        g_hidden_s[g] = g_hidden
        g_scal = dot_nn(w_env[...], g_hidden)
        rows_s[g, 6:7] = value
        for m in range(3):
            rows_s[g, 8 + m : 9 + m] = jnp.sum(g_scal * seen[(m + 1) * ch : (m + 2) * ch], 0, keepdims=True)
        spread = jnp.concatenate([g_scal] + [g_scal * harm[m] for m in range(3)], 0)
        scattered(g_gamma, spread, c_rows, blocks)
        return carry

    lax.fori_loop(0, groups, middle, 0)

    def backward(g, carry):
        blocks = pl.multiple_of(g * GROUP, GROUP)
        c_rows = centers[0, 0, pl.ds(blocks, GROUP), :] & (slots - 1)
        n_all = neighbours[0, 0, pl.ds(blocks, GROUP), :]
        n_rows = n_all & (slots - 1)
        n_cells = n_all >> 7
        back = gathered(g_gamma, c_rows, blocks)
        harm = [rows_s[g, m : m + 1] for m in range(3)]
        weight = rows_s[g, 3:4]
        scaled = rows_s[g, 4:5]
        inverse = rows_s[g, 5:6]
        value = rows_s[g, 6:7]
        chan = chan_s[g]
        g_weight = value
        g_chan = jnp.zeros_like(chan)
        g_harm = []
        for m in range(4):
            part = back[m * ch : (m + 1) * ch]
            along = jnp.sum(chan * part, 0, keepdims=True)
            if m == 0:
                g_weight = g_weight + along
                g_chan = g_chan + part
            else:
                g_weight = g_weight + along * harm[m - 1]
                g_chan = g_chan + part * harm[m - 1]
                g_harm.append(rows_s[g, 7 + m : 8 + m] + weight * along)
        g_chan = (g_chan * weight).astype(BF16)
        g_latent = dot_nn(w_mix[...], g_hidden_s[g]) + dot_nn(w_tensor[...], g_chan)
        g_zeta = dot_nn(w_latent[...], (g_latent * slope_l[g]).astype(BF16))
        g_pair = dot_nn(wr_bwd, (g_zeta * slope_z[g]).astype(BF16))
        _, cosines = sine_cosine(orders * scaled)
        turning = (3.14159265358979 * orders) * cosines
        g_scaled = jnp.sum((g_pair[:nb] + g_pair[nb:]) * turning, 0, keepdims=True)
        g_scaled = jnp.where(scaled < 1.0, g_scaled, 0.0)
        g_scaled = g_scaled - 4.0 * scaled * (1.0 - scaled * scaled) * g_weight
        radial = g_harm[0] * harm[0] + g_harm[1] * harm[1] + g_harm[2] * harm[2]
        pull = g_scaled * (1.0 / CUTOFF) - radial * inverse
        grads = [g_harm[m] * inverse + harm[m] * pull for m in range(3)]
        four = jnp.concatenate(grads + [weight * value], 0)
        high, low = split(four)
        eight = jnp.concatenate([high, low], 0)
        eight_n = eight * force_rows
        for j in range(GROUP):
            _, ext = cell_of(blocks + j)
            push[ext] += dot_nt(lanes(eight, j).astype(BF16), hot(c_rows[j : j + 1]))
            mine = lanes(eight_n, j)
            n_cell = n_cells[j : j + 1] - ext
            spread = jnp.concatenate([jnp.where(n_cell == offset, mine, 0.0) for offset in offsets], 0)
            out = dot_nt(spread.astype(BF16), hot(n_rows[j : j + 1]))
            for i, offset in enumerate(offsets):
                push[ext + offset] -= out[8 * i : 8 * i + 8]
        return carry

    lax.fori_loop(0, groups, backward, 0)

    for x in range(inner_x + 2):
        for y in range(wide_y):
            both = push[x * wide_y + y]
            total = both[0:4] + both[4:8]
            if x == 0:
                push_west[y] = total[:3]
            elif x == inner_x + 1:
                push_east[y] = total[:3]
            else:
                push_inner[x - 1, y] = total[:3]
                if 1 <= y <= inner_y:
                    energies[x - 1, y - 1 : y] = total[3:4]


def brick(centers, neighbours, live_blocks, table_c, packed, west, east, south, north, *weights):
    inner_x, inner_y, rows, slots = packed.shape
    blocks = centers.shape[2]
    lat = table_c.shape[1]
    ch = weights[2].shape[1]
    wide_y = inner_y + 2
    cells_ext = (inner_x + 2) * wide_y
    groups = blocks // GROUP
    width = GROUP * slots
    vmem = pl.BlockSpec(memory_space=pltpu.VMEM)
    smem = pl.BlockSpec(memory_space=pltpu.SMEM)
    anywhere = pl.BlockSpec(memory_space=pl.ANY)
    return pl.pallas_call(
        brick_kernel,
        in_specs=[smem, smem, vmem, vmem, vmem] + [anywhere] * 5 + [vmem] * 6,
        out_specs=(vmem,) * 4,
        out_shape=(
            jax.ShapeDtypeStruct((inner_x, inner_y, slots), F32),
            jax.ShapeDtypeStruct((wide_y, 3, slots), F32),
            jax.ShapeDtypeStruct((wide_y, 3, slots), F32),
            jax.ShapeDtypeStruct((inner_x, wide_y, 3, slots), F32),
        ),
        scratch_shapes=[
            pltpu.VMEM((cells_ext, rows, slots), F32),
            pltpu.VMEM((inner_x * inner_y, 4 * ch, slots), F32),
            pltpu.VMEM((inner_x * inner_y, 4 * ch, slots), F32),
            pltpu.VMEM((cells_ext, 8, slots), F32),
            pltpu.VMEM((groups, lat, width), F32),
            pltpu.VMEM((groups, lat, width), F32),
            pltpu.VMEM((groups, lat, width), BF16),
            pltpu.VMEM((groups, lat, width), BF16),
            pltpu.VMEM((groups, ch, width), F32),
            pltpu.VMEM((groups, 16, width), F32),
            pltpu.SemaphoreType.DMA((inner_x + 2 + 2 * (inner_x + 2),)),
        ],
        compiler_params=pltpu.CompilerParams(vmem_limit_bytes=40 * 1024 * 1024),
    )(centers, live_blocks, centers, neighbours, table_c, packed, west, east, south, north, *weights)


def body(
    features,
    coords,
    centers,
    neighbours,
    live_blocks,
    w_center,
    w_neigh,
    w_radial,
    w_latent,
    w_tensor,
    w_mix,
    w_env,
    w_out,
):
    table_c, packed = tables(features, coords, w_center, w_neigh)
    inner_x, inner_y = packed.shape[:2]
    west = shifted(packed[inner_x - 1 :], "bx", 1)
    east = shifted(packed[:1], "bx", -1)
    top = jnp.concatenate([west[:, inner_y - 1], packed[:, inner_y - 1], east[:, inner_y - 1]], 0)
    bottom = jnp.concatenate([west[:, 0], packed[:, 0], east[:, 0]], 0)
    south = shifted(top[:, None], "by", 1)
    north = shifted(bottom[:, None], "by", -1)
    weights = (w_radial, w_latent, w_tensor, w_mix, w_env, w_out[:, None])
    energies, push_west, push_east, inner = brick(
        centers, neighbours, live_blocks, table_c, packed, west, east, south, north, *weights
    )
    from_east = shifted(push_west, "bx", -1)
    from_west = shifted(push_east, "bx", 1)
    inner = inner.at[inner_x - 1].add(from_east).at[0].add(from_west)
    from_north = shifted(inner[:, 0], "by", -1)
    from_south = shifted(inner[:, inner_y + 1], "by", 1)
    forces = inner[:, 1 : inner_y + 1]
    forces = forces.at[:, inner_y - 1].add(from_north).at[:, 0].add(from_south)
    return (energies, forces)


def solution(mesh):
    split_both = P("bx", "by", None, None)
    placed = (split_both,) * 4 + (P("bx", "by"),) + (P(),) * 8
    return jax.shard_map(
        body,
        mesh=mesh,
        in_specs=placed,
        out_specs=(P("bx", "by", None), split_both),
        check_vma=False,
    )
```

time: 309 us -> 75.7 us (0.24)
  the two profiles are of different devices: /device:TPU:1 before, /device:TPU:6 now
where the time goes in v1:
time: 75.7 us; the launch traced here: 75.2 us
  starting transfers between devices  44.6 us (59%)
  waiting for transfers between devices  19 us (25%)
  Pallas kernels  7.18 us (9%)
  local copies, waits for them, and re-layouts  2.74 us (4%)
  between operations  1.58 us (2%)
    ppermute x8, starting transfers between devices, shifted(): lax.ppermute(array, axis, [(i, (i + by) % length) for i in range(length)])  44.6 us
    ppermute x8, waiting for transfers between devices, shifted(): lax.ppermute(array, axis, [(i, (i + by) % length) for i in range(length)])  19 us
    pallas_call x1, Pallas kernels, brick(): pl.pallas_call(brick_kernel, in_specs=[smem, smem, vmem, vmem, vmem] + [a...  6.78 us
    unnamed x26, local copies, waits for them, and re-layouts  2.58 us
  transfers between devices with their start and end apart: 8, of which 6 were waited for; matrix products, arithmetic and copies ran while one was open for 0% of the time, Pallas kernels for 0%

profile of v1, /device:TPU:6, one launch (start us, length us, event | category | flops | bytes accessed | tf_op | source)
XLA Modules:
  0.0 75.2 jit_solution(18420724524316550232)
XLA Ops:
  0.6 0.0 copy-start.5
  0.6 0.0 copy-start.6
  0.7 0.8 %copy.15.coord = f32[4,4,3,128]{3,2,1,0:T(4,128)S(1)} copy(f32[4,4,3,128]{3,1,2,0:T(4,128)} %param.22) | data formatting | bytes 49152 | tf_op args[1]
  1.4 0.0 copy-done.5
  1.4 0.0 copy-done.6
  1.4 0.0 copy-start
  1.4 1.0 %copy-done = f32[4,4,64,128]{3,2,1,0:T(8,128)S(1)} copy-done((f32[4,4,64,128]{3,2,1,0:T(8,128)S(1)}, f32[4,4,64,128]{3,2,1,0:T(8,128)}, u32[]{:S(2)}) %copy-start) | copy-done | bytes 524312
  2.5 0.4 shard_map.140
  2.9 4.3 %collective-permute-start = (f32[1,4,72,128]{3,2,1,0:T(8,128)S(1)}, f32[1,4,72,128]{3,2,1,0:T(8,128)S(1)}, u32[]{:S(2)}, u32[]{:S(2)}) collective-permute-start(f32[1,4,72,128]{3,2,1,0:T(8,128)S(1)} %get-tuple-element.67), channel_id=1, source_target_pairs={{0,64},{64,128},{128,192},{192,256},{256,320},{320,384},{384,448},... | collective-permute-start | bytes 442376 | tf_op jit(solution)/shard_map/ppermute | solution.py:21
  7.2 12.2 %collective-permute-start.1 = (f32[1,4,72,128]{3,2,1,0:T(8,128)S(1)}, f32[1,4,72,128]{3,2,1,0:T(8,128)S(1)}, u32[]{:S(2)}, u32[]{:S(2)}) collective-permute-start(f32[1,4,72,128]{3,2,1,0:T(8,128)S(1)} %get-tuple-element.66), channel_id=1, source_target_pairs={{0,704},{64,0},{128,64},{192,128},{256,192},{320,256},{384,320},{4... | collective-permute-start | bytes 442376 | tf_op jit(solution)/shard_map/ppermute | solution.py:21
  19.5 1.9 %collective-permute-done.west = f32[1,4,72,128]{3,2,1,0:T(8,128)S(1)} collective-permute-done((f32[1,4,72,128]{3,2,1,0:T(8,128)S(1)}, f32[1,4,72,128]{3,2,1,0:T(8,128)S(1)}, u32[]{:S(2)}, u32[]{:S(2)}) %collective-permute-start) | collective-permute-done | bytes 147488 | tf_op jit(solution)/shard_map/ppermute | solution.py:21
  21.3 1.2 %collective-permute-done.1.east = f32[1,4,72,128]{3,2,1,0:T(8,128)S(1)} collective-permute-done((f32[1,4,72,128]{3,2,1,0:T(8,128)S(1)}, f32[1,4,72,128]{3,2,1,0:T(8,128)S(1)}, u32[]{:S(2)}, u32[]{:S(2)}) %collective-permute-start.1) | collective-permute-done | bytes 147488 | tf_op jit(solution)/shard_map/ppermute | solution.py:21
  22.5 4.2 %collective-permute-start.3 = (f32[6,1,72,128]{3,2,1,0:T(8,128)S(1)}, f32[6,1,72,128]{3,2,1,0:T(8,128)S(1)}, u32[]{:S(2)}, u32[]{:S(2)}) collective-permute-start(f32[6,1,72,128]{3,2,1,0:T(8,128)S(1)} %maximum_bitcast_fusion.1), channel_id=1, source_target_pairs={{0,63},{1,0},{2,1},{3,2},{4,3},{5,4},{6,5},{7,6},{8,7},{9,8},{10,9... | collective-permute-start | bytes 663560 | tf_op jit(solution)/shard_map/ppermute | solution.py:21
  26.8 0.0 copy-start.9
  26.8 0.0 copy-start.4
  26.8 0.0 copy-start.10
  26.8 1.9 %collective-permute-start.2 = (f32[6,1,72,128]{3,2,1,0:T(8,128)S(1)}, f32[6,1,72,128]{3,2,1,0:T(8,128)S(1)}, u32[]{:S(2)}, u32[]{:S(2)}) collective-permute-start(f32[6,1,72,128]{3,2,1,0:T(8,128)S(1)} %maximum_bitcast_fusion), channel_id=1, source_target_pairs={{0,1},{1,2},{2,3},{3,4},{4,5},{5,6},{6,7},{7,8},{8,9},{9,10},{10,1... | collective-permute-start | bytes 663560 | tf_op jit(solution)/shard_map/ppermute | solution.py:21
  28.8 0.0 copy-done.10
  28.8 0.0 copy-start.2
  28.8 0.0 copy-start.3
  28.8 0.0 copy-start.8
  28.8 0.1 copy.19.w_out
  28.9 0.0 copy-done.9
  28.9 0.0 copy-start.1
  28.9 0.0 copy-start.7
  28.9 0.1 copy.18.w_tensor
  29.7 0.5 collective-permute-done.3.north
  30.2 6.0 %collective-permute-done.2.south = f32[6,1,72,128]{3,2,1,0:T(8,128)S(1)} collective-permute-done((f32[6,1,72,128]{3,2,1,0:T(8,128)S(1)}, f32[6,1,72,128]{3,2,1,0:T(8,128)S(1)}, u32[]{:S(2)}, u32[]{:S(2)}) %collective-permute-start.2) | collective-permute-done | bytes 221216 | tf_op jit(solution)/shard_map/ppermute | solution.py:21
  36.2 0.0 copy-done.4
  36.2 0.0 copy-done.2
  36.2 0.0 copy-done.3
  36.2 0.0 copy-done.8
  36.2 0.0 copy-done.1
  36.2 0.0 copy-done.7
  36.2 6.8 %shard_map.141 = (f32[4,4,128]{2,1,0:T(4,128)}, f32[6,3,128]{2,1,0:T(4,128)S(1)}, f32[6,3,128]{2,1,0:T(4,128)S(1)}, f32[4,6,3,128]{3,2,1,0:T(4,128)S(1)}) custom-call(s32[1,1,32,128]{3,2,1,0:T(8,128)S(1)} %copy-done.1, s32[1,1]{1,0:T(1,128)S(6)} %copy.33.live, s32[1,1,32,128]{3,2,1,0:T(8,128)S(1)} %copy-done.1, s32[1,1,32,128]{3,2,1,0:T(8,128)S(1)} %copy-done.2, ...), custom_call_target="tpu_custom_call" | custom-call | tf_op jit(solution)/shard_map/pallas_call | solution.py:348
  43.0 15.7 %collective-permute-start.4 = (f32[6,3,128]{2,1,0:T(4,128)S(1)}, f32[6,3,128]{2,1,0:T(4,128)S(1)}, u32[]{:S(2)}, u32[]{:S(2)}) collective-permute-start(f32[6,3,128]{2,1,0:T(4,128)S(1)} %get-tuple-element.60), channel_id=1, source_target_pairs={{0,704},{64,0},{128,64},{192,128},{256,192},{320,256},{384,320},{4... | collective-permute-start | bytes 27656 | tf_op jit(solution)/shard_map/ppermute | solution.py:21
  58.7 1.9 %collective-permute-start.5 = (f32[6,3,128]{2,1,0:T(4,128)S(1)}, f32[6,3,128]{2,1,0:T(4,128)S(1)}, u32[]{:S(2)}, u32[]{:S(2)}) collective-permute-start(f32[6,3,128]{2,1,0:T(4,128)S(1)} %get-tuple-element.61), channel_id=1, source_target_pairs={{0,64},{64,128},{128,192},{192,256},{256,320},{320,384},{384,448},... | collective-permute-start | bytes 27656 | tf_op jit(solution)/shard_map/ppermute | solution.py:21
  60.6 0.0 collective-permute-done.4
  60.7 4.8 %collective-permute-done.5 = f32[6,3,128]{2,1,0:T(4,128)S(1)} collective-permute-done((f32[6,3,128]{2,1,0:T(4,128)S(1)}, f32[6,3,128]{2,1,0:T(4,128)S(1)}, u32[]{:S(2)}, u32[]{:S(2)}) %collective-permute-start.5) | collective-permute-done | bytes 9248 | tf_op jit(solution)/shard_map/ppermute | solution.py:21
  65.5 1.9 %collective-permute-start.6 = (f32[4,3,128]{2,1,0:T(4,128)S(1)}, f32[4,3,128]{2,1,0:T(4,128)S(1)}, u32[]{:S(2)}, u32[]{:S(2)}) collective-permute-start(f32[4,3,128]{2,1,0:T(4,128)S(1)} %get-tuple-element.73), channel_id=1, source_target_pairs={{0,63},{1,0},{2,1},{3,2},{4,3},{5,4},{6,5},{7,6},{8,7},{9,8},{10,9... | collective-permute-start | bytes 18440 | tf_op jit(solution)/shard_map/ppermute | solution.py:21
  67.5 2.4 %collective-permute-start.7 = (f32[4,3,128]{2,1,0:T(4,128)S(1)}, f32[4,3,128]{2,1,0:T(4,128)S(1)}, u32[]{:S(2)}, u32[]{:S(2)}) collective-permute-start(f32[4,3,128]{2,1,0:T(4,128)S(1)} %get-tuple-element.72), channel_id=1, source_target_pairs={{0,1},{1,2},{2,3},{3,4},{4,5},{5,6},{6,7},{7,8},{8,9},{9,10},{10,1... | collective-permute-start | bytes 18440 | tf_op jit(solution)/shard_map/ppermute | solution.py:21
  69.9 0.0 collective-permute-done.6
  69.9 4.6 %collective-permute-done.7 = f32[4,3,128]{2,1,0:T(4,128)S(1)} collective-permute-done((f32[4,3,128]{2,1,0:T(4,128)S(1)}, f32[4,3,128]{2,1,0:T(4,128)S(1)}, u32[]{:S(2)}, u32[]{:S(2)}) %collective-permute-start.7) | collective-permute-done | bytes 6176 | tf_op jit(solution)/shard_map/ppermute | solution.py:21
  74.6 0.6 copy.23
  (13 shorter events, 0.2 us)
Async XLA Ops:
  0.6 0.8 %copy-start.5 = (bf16[64,64]{1,0:T(8,128)(2,1)S(1)}, bf16[64,64]{1,0:T(8,128)(2,1)}, u32[]{:S(2)}) copy-start(bf16[64,64]{1,0:T(8,128)(2,1)} %w_center.1) | copy-start | bytes 24580
  0.6 0.8 %copy-start.6 = (bf16[64,64]{1,0:T(8,128)(2,1)S(1)}, bf16[64,64]{1,0:T(8,128)(2,1)}, u32[]{:S(2)}) copy-start(bf16[64,64]{1,0:T(8,128)(2,1)} %w_neigh.1) | copy-start | bytes 24580
  1.4 1.0 %copy-start = (f32[4,4,64,128]{3,2,1,0:T(8,128)S(1)}, f32[4,4,64,128]{3,2,1,0:T(8,128)}, u32[]{:S(2)}) copy-start(f32[4,4,64,128]{3,2,1,0:T(8,128)} %feat.1) | copy-start | bytes 1572868
  2.9 18.4 %collective-permute-start = (f32[1,4,72,128]{3,2,1,0:T(8,128)S(1)}, f32[1,4,72,128]{3,2,1,0:T(8,128)S(1)}, u32[]{:S(2)}, u32[]{:S(2)}) collective-permute-start(f32[1,4,72,128]{3,2,1,0:T(8,128)S(1)} %get-tuple-element.67), channel_id=1, source_target_pairs={{0,64},{64,128},{128,192},{192,256},{256,320},{320,384},{384,448},... | collective-permute-start | bytes 442376 | tf_op jit(solution)/shard_map/ppermute | solution.py:21
  7.2 15.3 %collective-permute-start.1 = (f32[1,4,72,128]{3,2,1,0:T(8,128)S(1)}, f32[1,4,72,128]{3,2,1,0:T(8,128)S(1)}, u32[]{:S(2)}, u32[]{:S(2)}) collective-permute-start(f32[1,4,72,128]{3,2,1,0:T(8,128)S(1)} %get-tuple-element.66), channel_id=1, source_target_pairs={{0,704},{64,0},{128,64},{192,128},{256,192},{320,256},{384,320},{4... | collective-permute-start | bytes 442376 | tf_op jit(solution)/shard_map/ppermute | solution.py:21
  22.5 7.6 %collective-permute-start.3 = (f32[6,1,72,128]{3,2,1,0:T(8,128)S(1)}, f32[6,1,72,128]{3,2,1,0:T(8,128)S(1)}, u32[]{:S(2)}, u32[]{:S(2)}) collective-permute-start(f32[6,1,72,128]{3,2,1,0:T(8,128)S(1)} %maximum_bitcast_fusion.1), channel_id=1, source_target_pairs={{0,63},{1,0},{2,1},{3,2},{4,3},{5,4},{6,5},{7,6},{8,7},{9,8},{10,9... | collective-permute-start | bytes 663560 | tf_op jit(solution)/shard_map/ppermute | solution.py:21
  26.8 2.1 %copy-start.9 = (bf16[64,16]{0,1:T(8,128)(2,1)S(1)}, bf16[64,16]{0,1:T(8,128)(2,1)}, u32[]{:S(2)}) copy-start(bf16[64,16]{0,1:T(8,128)(2,1)} %param.30) | copy-start | bytes 6148
  26.8 9.4 %copy-start.4 = (bf16[64,64]{1,0:T(8,128)(2,1)S(1)}, bf16[64,64]{1,0:T(8,128)(2,1)}, u32[]{:S(2)}) copy-start(bf16[64,64]{1,0:T(8,128)(2,1)} %w_mix.1) | copy-start | bytes 24580
  26.8 1.9 %copy-start.10 = (f32[64]{0:T(128)S(1)}, f32[64]{0:T(128)}, u32[]{:S(2)}) copy-start(f32[64]{0:T(128)} %param.33) | copy-start | bytes 772
  26.8 9.4 %collective-permute-start.2 = (f32[6,1,72,128]{3,2,1,0:T(8,128)S(1)}, f32[6,1,72,128]{3,2,1,0:T(8,128)S(1)}, u32[]{:S(2)}, u32[]{:S(2)}) collective-permute-start(f32[6,1,72,128]{3,2,1,0:T(8,128)S(1)} %maximum_bitcast_fusion), channel_id=1, source_target_pairs={{0,1},{1,2},{2,3},{3,4},{4,5},{5,6},{6,7},{7,8},{8,9},{9,10},{10,1... | collective-permute-start | bytes 663560 | tf_op jit(solution)/shard_map/ppermute | solution.py:21
  28.8 7.4 %copy-start.2 = (s32[1,1,32,128]{3,2,1,0:T(8,128)S(1)}, s32[1,1,32,128]{3,2,1,0:T(8,128)}, u32[]{:S(2)}) copy-start(s32[1,1,32,128]{3,2,1,0:T(8,128)} %neighbours.1) | copy-start | bytes 49156
  28.8 7.4 %copy-start.3 = (bf16[64,64]{1,0:T(8,128)(2,1)S(1)}, bf16[64,64]{1,0:T(8,128)(2,1)}, u32[]{:S(2)}) copy-start(bf16[64,64]{1,0:T(8,128)(2,1)} %w_latent.1) | copy-start | bytes 24580
  28.8 7.4 %copy-start.8 = (bf16[16,64]{1,0:T(8,128)(2,1)S(1)}, bf16[16,64]{1,0:T(8,128)(2,1)}, u32[]{:S(2)}) copy-start(bf16[16,64]{1,0:T(8,128)(2,1)} %w_env.1) | copy-start | bytes 6148
  28.9 7.3 %copy-start.1 = (s32[1,1,32,128]{3,2,1,0:T(8,128)S(1)}, s32[1,1,32,128]{3,2,1,0:T(8,128)}, u32[]{:S(2)}) copy-start(s32[1,1,32,128]{3,2,1,0:T(8,128)} %centers.1) | copy-start | bytes 49156
  28.9 7.3 %copy-start.7 = (f32[8,64]{1,0:T(8,128)S(1)}, f32[8,64]{1,0:T(8,128)}, u32[]{:S(2)}) copy-start(f32[8,64]{1,0:T(8,128)} %w_radial.1) | copy-start | bytes 6148
  43.0 17.6 %collective-permute-start.4 = (f32[6,3,128]{2,1,0:T(4,128)S(1)}, f32[6,3,128]{2,1,0:T(4,128)S(1)}, u32[]{:S(2)}, u32[]{:S(2)}) collective-permute-start(f32[6,3,128]{2,1,0:T(4,128)S(1)} %get-tuple-element.60), channel_id=1, source_target_pairs={{0,704},{64,0},{128,64},{192,128},{256,192},{320,256},{384,320},{4... | collective-permute-start | bytes 27656 | tf_op jit(solution)/shard_map/ppermute | solution.py:21
  58.7 6.8 %collective-permute-start.5 = (f32[6,3,128]{2,1,0:T(4,128)S(1)}, f32[6,3,128]{2,1,0:T(4,128)S(1)}, u32[]{:S(2)}, u32[]{:S(2)}) collective-permute-start(f32[6,3,128]{2,1,0:T(4,128)S(1)} %get-tuple-element.61), channel_id=1, source_target_pairs={{0,64},{64,128},{128,192},{192,256},{256,320},{320,384},{384,448},... | collective-permute-start | bytes 27656 | tf_op jit(solution)/shard_map/ppermute | solution.py:21
  65.5 4.4 %collective-permute-start.6 = (f32[4,3,128]{2,1,0:T(4,128)S(1)}, f32[4,3,128]{2,1,0:T(4,128)S(1)}, u32[]{:S(2)}, u32[]{:S(2)}) collective-permute-start(f32[4,3,128]{2,1,0:T(4,128)S(1)} %get-tuple-element.73), channel_id=1, source_target_pairs={{0,63},{1,0},{2,1},{3,2},{4,3},{5,4},{6,5},{7,6},{8,7},{9,8},{10,9... | collective-permute-start | bytes 18440 | tf_op jit(solution)/shard_map/ppermute | solution.py:21
  67.5 7.1 %collective-permute-start.7 = (f32[4,3,128]{2,1,0:T(4,128)S(1)}, f32[4,3,128]{2,1,0:T(4,128)S(1)}, u32[]{:S(2)}, u32[]{:S(2)}) collective-permute-start(f32[4,3,128]{2,1,0:T(4,128)S(1)} %get-tuple-element.72), channel_id=1, source_target_pairs={{0,1},{1,2},{2,3},{3,4},{4,5},{5,6},{6,7},{7,8},{8,9},{9,10},{10,1... | collective-permute-start | bytes 18440 | tf_op jit(solution)/shard_map/ppermute | solution.py:21

commit v2 on v1

--- a/solution.py
+++ b/solution.py
@@ -9,7 +9,7 @@
 CUTOFF = 6.0
 SOFTEN = 0.25
 ROWS = 72
-GROUP = 8
+GROUP = 32
 F32 = jnp.float32
 BF16 = jnp.bfloat16
 SIN_TERMS = (3.14159265358979, -5.16771278004997, 2.55016403987735, -0.599264529320792, 0.0821458866111282, -0.00737043094571435)
@@ -40,7 +40,7 @@
 
 def tables_kernel(feat, coord, w_center, w_neigh, table_c, packed):
     inner_x, inner_y, lat, slots = feat.shape
-    both = jnp.concatenate([w_center[...].astype(F32), w_neigh[...].astype(F32)], 1)
+    both = 0.5 * jnp.concatenate([w_center[...].astype(F32), w_neigh[...].astype(F32)], 1)
     both = jnp.concatenate([both, both], 0).T.astype(BF16)
     pad = jnp.zeros((ROWS - lat - 3, slots), F32)
     for x in range(inner_x):
@@ -51,7 +51,7 @@
             piece = out[:, y * slots : (y + 1) * slots]
             table_c[x * inner_y + y] = piece[:lat]
             packed[x, y, :lat] = piece[lat:]
-            packed[x, y, lat:] = jnp.concatenate([coord[x, y], pad], 0)
+            packed[x, y, lat:] = jnp.concatenate([coord[x, m, y : y + 1] for m in range(3)] + [pad], 0)
 
 
 def tables(features, coords, w_center, w_neigh):
@@ -81,10 +81,14 @@
     return sign * part * poly(SIN_TERMS), sign * poly(COS_TERMS)
 
 
-def gated(value):
-    gate = 0.5 * jnp.tanh(0.5 * value) + 0.5
-    silu = value * gate
-    return silu, gate + silu - silu * gate
+def gated(half):
+    gate = 1.0 + jnp.tanh(half)
+    silu = half * gate
+    return silu, gate + silu * (2.0 - gate)
+
+
+def halved(array):
+    return (array.astype(F32) * 0.5).astype(array.dtype)
 
 
 def brick_kernel(
@@ -118,7 +122,6 @@
     g_hidden_s,
     chan_s,
     rows_s,
-    sems,
 ):
     inner_x, inner_y, _, slots = packed.shape
     wide_y = inner_y + 2
@@ -126,24 +129,24 @@
     ch = w_tensor.shape[1]
     nb = w_radial.shape[0]
     width = GROUP * slots
-    copies = []
-    for x in range(inner_x):
-        copies.append((packed.at[x], (x + 1) * wide_y + 1, inner_y))
-    copies.append((west.at[0], 1, inner_y))
-    copies.append((east.at[0], (inner_x + 1) * wide_y + 1, inner_y))
     for x in range(inner_x + 2):
-        copies.append((south.at[x], x * wide_y, 1))
-        copies.append((north.at[x], x * wide_y + inner_y + 1, 1))
-    started = []
-    for i, (source, at, count) in enumerate(copies):
-        copy = pltpu.make_async_copy(source, table_n.at[pl.ds(at, count)], sems.at[i])
-        copy.start()
-        started.append(copy)
-
+        for y in range(wide_y):
+            if y == 0:
+                source = south[x, 0]
+            elif y == inner_y + 1:
+                source = north[x, 0]
+            elif x == 0:
+                source = west[0, y - 1]
+            elif x == inner_x + 1:
+                source = east[0, y - 1]
+            else:
+                source = packed[x - 1, y - 1]
+            table_n[x * wide_y + y] = source
     gamma[...] = jnp.zeros_like(gamma)
     g_gamma[...] = jnp.zeros_like(g_gamma)
     push[...] = jnp.zeros_like(push)
-    wr_high, wr_low = split(w_radial[...])
+    wr_high, wr_low = split(0.5 * w_radial[...])
+    half_latent, half_mix, half_env = halved(w_latent[...]), halved(w_mix[...]), halved(w_env[...])
     wr_fwd = jnp.concatenate([wr_high, wr_high, wr_low, wr_low], 0).astype(BF16)
     wr_bwd = jnp.concatenate([wr_high, wr_low], 0).astype(BF16)
     orders = lax.broadcasted_iota(jnp.int32, (nb, 1), 0).astype(F32) + 1.0
@@ -151,13 +154,13 @@
     row_iota = lax.broadcasted_iota(jnp.int32, (8, 1), 0)
     force_rows = jnp.where((row_iota & 3) == 3, 0.0, 1.0)
     out_col = w_out[...]
+    half_col = 0.5 * out_col
     offsets = [dx * wide_y + dy for dx in (-1, 0, 1) for dy in (-1, 0, 1)]
-    groups = live[0, 0] // GROUP
-    for copy in started:
-        copy.wait()
+    groups = (live[0, 0] + (GROUP - 1)) // GROUP
+    block_iota = lax.broadcasted_iota(jnp.int32, (1, width), 1) // slots
 
     def cell_of(block):
-        cell = cells[0, 0, block, 0] // slots
+        cell = cells[0, block] // slots
         cell_x = cell // inner_y
         return cell, (cell_x + 1) * wide_y + (cell - cell_x * inner_y) + 1
 
@@ -216,14 +219,14 @@
         inverse = lax.rsqrt(length2)
         scaled = jnp.minimum(length2 * inverse * (1.0 / CUTOFF), 1.0)
         fall = 1.0 - scaled * scaled
-        weight = fall * fall
+        weight = jnp.where(block_iota + blocks < live[0, 0], fall * fall, 0.0)
         harm = delta * inverse
         basis, _ = sine_cosine(orders * scaled)
         b_high, b_low = split(basis)
         b_all = jnp.concatenate([b_high, b_low, b_high, b_low], 0).astype(BF16)
         zeta, slope = gated(near + dot_tn(wr_fwd, b_all))
         slope_z[g] = slope
-        latent, slope = gated(dot_tn(w_latent[...], zeta.astype(BF16)))
+        latent, slope = gated(dot_tn(half_latent, zeta.astype(BF16)))
         slope_l[g] = slope
         latent = latent.astype(BF16)
         latent_s[g] = latent
@@ -249,10 +252,10 @@
         scal = seen[:ch]
         for m in range(3):
             scal = scal + harm[m] * seen[(m + 1) * ch : (m + 2) * ch]
-        hidden = dot_tn(w_mix[...], latent_s[g]) + dot_tn(w_env[...], scal.astype(BF16))
+        hidden = dot_tn(half_mix, latent_s[g]) + dot_tn(half_env, scal.astype(BF16))
         lifted, slope = gated(hidden)
         value = jnp.sum(out_col * lifted, 0, keepdims=True)
-        g_hidden = ((out_col * slope) * weight).astype(BF16)
+        g_hidden = ((half_col * slope) * weight).astype(BF16)
         g_hidden_s[g] = g_hidden
         g_scal = dot_nn(w_env[...], g_hidden)
         rows_s[g, 6:7] = value
@@ -292,12 +295,13 @@
                 g_harm.append(rows_s[g, 7 + m : 8 + m] + weight * along)
         g_chan = (g_chan * weight).astype(BF16)
         g_latent = dot_nn(w_mix[...], g_hidden_s[g]) + dot_nn(w_tensor[...], g_chan)
-        g_zeta = dot_nn(w_latent[...], (g_latent * slope_l[g]).astype(BF16))
+        g_zeta = dot_nn(half_latent, (g_latent * slope_l[g]).astype(BF16))
         g_pair = dot_nn(wr_bwd, (g_zeta * slope_z[g]).astype(BF16))
         _, cosines = sine_cosine(orders * scaled)
         turning = (3.14159265358979 * orders) * cosines
         g_scaled = jnp.sum((g_pair[:nb] + g_pair[nb:]) * turning, 0, keepdims=True)
         g_scaled = jnp.where(scaled < 1.0, g_scaled, 0.0)
+        g_weight = jnp.where(block_iota + blocks < live[0, 0], g_weight, 0.0)
         g_scaled = g_scaled - 4.0 * scaled * (1.0 - scaled * scaled) * g_weight
         radial = g_harm[0] * harm[0] + g_harm[1] * harm[1] + g_harm[2] * harm[2]
         pull = g_scaled * (1.0 / CUTOFF) - radial * inverse
@@ -323,14 +327,15 @@
         for y in range(wide_y):
             both = push[x * wide_y + y]
             total = both[0:4] + both[4:8]
-            if x == 0:
-                push_west[y] = total[:3]
-            elif x == inner_x + 1:
-                push_east[y] = total[:3]
-            else:
-                push_inner[x - 1, y] = total[:3]
-                if 1 <= y <= inner_y:
-                    energies[x - 1, y - 1 : y] = total[3:4]
+            for m in range(3):
+                if x == 0:
+                    push_west[m, y : y + 1] = total[m : m + 1]
+                elif x == inner_x + 1:
+                    push_east[m, y : y + 1] = total[m : m + 1]
+                else:
+                    push_inner[x - 1, m, y : y + 1] = total[m : m + 1]
+            if 1 <= x <= inner_x and 1 <= y <= inner_y:
+                energies[x - 1, y - 1 : y] = total[3:4]
 
 
 def brick(centers, neighbours, live_blocks, table_c, packed, west, east, south, north, *weights):
@@ -344,16 +349,15 @@
     width = GROUP * slots
     vmem = pl.BlockSpec(memory_space=pltpu.VMEM)
     smem = pl.BlockSpec(memory_space=pltpu.SMEM)
-    anywhere = pl.BlockSpec(memory_space=pl.ANY)
     return pl.pallas_call(
         brick_kernel,
-        in_specs=[smem, smem, vmem, vmem, vmem] + [anywhere] * 5 + [vmem] * 6,
+        in_specs=[smem, smem] + [vmem] * 14,
         out_specs=(vmem,) * 4,
         out_shape=(
             jax.ShapeDtypeStruct((inner_x, inner_y, slots), F32),
-            jax.ShapeDtypeStruct((wide_y, 3, slots), F32),
-            jax.ShapeDtypeStruct((wide_y, 3, slots), F32),
-            jax.ShapeDtypeStruct((inner_x, wide_y, 3, slots), F32),
+            jax.ShapeDtypeStruct((3, wide_y, slots), F32),
+            jax.ShapeDtypeStruct((3, wide_y, slots), F32),
+            jax.ShapeDtypeStruct((inner_x, 3, wide_y, slots), F32),
         ),
         scratch_shapes=[
             pltpu.VMEM((cells_ext, rows, slots), F32),
@@ -366,10 +370,9 @@
             pltpu.VMEM((groups, lat, width), BF16),
             pltpu.VMEM((groups, ch, width), F32),
             pltpu.VMEM((groups, 16, width), F32),
-            pltpu.SemaphoreType.DMA((inner_x + 2 + 2 * (inner_x + 2),)),
         ],
         compiler_params=pltpu.CompilerParams(vmem_limit_bytes=40 * 1024 * 1024),
-    )(centers, live_blocks, centers, neighbours, table_c, packed, west, east, south, north, *weights)
+    )(centers[0, :, :, 0], live_blocks, centers, neighbours, table_c, packed, west, east, south, north, *weights)
 
 
 def body(
@@ -387,7 +390,7 @@
     w_env,
     w_out,
 ):
-    table_c, packed = tables(features, coords, w_center, w_neigh)
+    table_c, packed = tables(features, jnp.swapaxes(coords, 1, 2), w_center, w_neigh)
     inner_x, inner_y = packed.shape[:2]
     west = shifted(packed[inner_x - 1 :], "bx", 1)
     east = shifted(packed[:1], "bx", -1)
@@ -402,10 +405,11 @@
     from_east = shifted(push_west, "bx", -1)
     from_west = shifted(push_east, "bx", 1)
     inner = inner.at[inner_x - 1].add(from_east).at[0].add(from_west)
-    from_north = shifted(inner[:, 0], "by", -1)
-    from_south = shifted(inner[:, inner_y + 1], "by", 1)
-    forces = inner[:, 1 : inner_y + 1]
-    forces = forces.at[:, inner_y - 1].add(from_north).at[:, 0].add(from_south)
+    from_north = shifted(inner[:, :, 0], "by", -1)
+    from_south = shifted(inner[:, :, inner_y + 1], "by", 1)
+    forces = inner[:, :, 1 : inner_y + 1]
+    forces = forces.at[:, :, inner_y - 1].add(from_north).at[:, :, 0].add(from_south)
+    forces = jnp.swapaxes(forces, 1, 2)
     return (energies, forces)
 
 

time: 75.7 us -> 71.9 us (0.950)
  the two profiles are of different devices: /device:TPU:6 before, /device:TPU:1 now
where the time goes in v2:
time: 71.9 us; the launch traced here: 71.2 us
  starting transfers between devices  43.8 us (61%)
  Pallas kernels  11.2 us (16%)
  waiting for transfers between devices  10.2 us (14%)
  local copies, waits for them, and re-layouts  4.34 us (6%)
  between operations  1.57 us (2%)
    ppermute x8, starting transfers between devices, shifted(): lax.ppermute(array, axis, [(i, (i + by) % length) for i in range(length)])  43.8 us
    pallas_call x1, Pallas kernels, brick(): pl.pallas_call(brick_kernel, in_specs=[smem, smem] + [vmem] * 14, out_spe...  10.8 us
    ppermute x8, waiting for transfers between devices, shifted(): lax.ppermute(array, axis, [(i, (i + by) % length) for i in range(length)])  10.2 us
    unnamed x27, local copies, waits for them, and re-layouts  3.95 us
  transfers between devices with their start and end apart: 8, of which 6 were waited for; matrix products, arithmetic and copies ran while one was open for 1% of the time, Pallas kernels for 0%

profile of v2, /device:TPU:1, one launch (start us, length us, event | category | flops | bytes accessed | tf_op | source)
XLA Modules:
  0.0 71.2 jit_solution(18342521924352574288)
XLA Ops:
  0.6 0.0 copy-start
  0.6 1.0 %copy-done = f32[4,4,64,128]{3,2,1,0:T(8,128)S(1)} copy-done((f32[4,4,64,128]{3,2,1,0:T(8,128)S(1)}, f32[4,4,64,128]{3,2,1,0:T(8,128)}, u32[]{:S(2)}) %copy-start) | copy-done | bytes 524312
  1.7 0.0 copy-start.2
  1.7 0.7 %copy-done.2 = f32[4,4,3,128]{3,1,2,0:T(4,128)S(1)} copy-done((f32[4,4,3,128]{3,1,2,0:T(4,128)S(1)}, f32[4,4,3,128]{3,1,2,0:T(4,128)}, u32[]{:S(2)}) %copy-start.2) | copy-done | bytes 24600
  2.4 0.0 copy-start.6
  2.4 0.7 %copy-done.6 = bf16[64,64]{1,0:T(8,128)(2,1)S(1)} copy-done((bf16[64,64]{1,0:T(8,128)(2,1)S(1)}, bf16[64,64]{1,0:T(8,128)(2,1)}, u32[]{:S(2)}) %copy-start.6) | copy-done | bytes 8216
  3.1 0.0 copy-start.7
  3.1 0.7 %copy-done.7 = bf16[64,64]{1,0:T(8,128)(2,1)S(1)} copy-done((bf16[64,64]{1,0:T(8,128)(2,1)S(1)}, bf16[64,64]{1,0:T(8,128)(2,1)}, u32[]{:S(2)}) %copy-start.7) | copy-done | bytes 8216
  3.8 0.4 shard_map.140
  4.3 4.8 %collective-permute-start = (f32[1,4,72,128]{3,2,1,0:T(8,128)S(1)}, f32[1,4,72,128]{3,2,1,0:T(8,128)S(1)}, u32[]{:S(2)}, u32[]{:S(2)}) collective-permute-start(f32[1,4,72,128]{3,2,1,0:T(8,128)S(1)} %get-tuple-element.67), channel_id=1, source_target_pairs={{0,64},{64,128},{128,192},{192,256},{256,320},{320,384},{384,448},... | collective-permute-start | bytes 442376 | tf_op jit(solution)/shard_map/ppermute | solution.py:21
  9.1 12.2 %collective-permute-start.1 = (f32[1,4,72,128]{3,2,1,0:T(8,128)S(1)}, f32[1,4,72,128]{3,2,1,0:T(8,128)S(1)}, u32[]{:S(2)}, u32[]{:S(2)}) collective-permute-start(f32[1,4,72,128]{3,2,1,0:T(8,128)S(1)} %get-tuple-element.66), channel_id=1, source_target_pairs={{0,704},{64,0},{128,64},{192,128},{256,192},{320,256},{384,320},{4... | collective-permute-start | bytes 442376 | tf_op jit(solution)/shard_map/ppermute | solution.py:21
  21.4 1.6 %collective-permute-done.west = f32[1,4,72,128]{3,2,1,0:T(8,128)S(1)} collective-permute-done((f32[1,4,72,128]{3,2,1,0:T(8,128)S(1)}, f32[1,4,72,128]{3,2,1,0:T(8,128)S(1)}, u32[]{:S(2)}, u32[]{:S(2)}) %collective-permute-start) | collective-permute-done | bytes 147488 | tf_op jit(solution)/shard_map/ppermute | solution.py:21
  23.0 0.9 %collective-permute-done.1.east = f32[1,4,72,128]{3,2,1,0:T(8,128)S(1)} collective-permute-done((f32[1,4,72,128]{3,2,1,0:T(8,128)S(1)}, f32[1,4,72,128]{3,2,1,0:T(8,128)S(1)}, u32[]{:S(2)}, u32[]{:S(2)}) %collective-permute-start.1) | collective-permute-done | bytes 147488 | tf_op jit(solution)/shard_map/ppermute | solution.py:21
  23.9 3.5 %collective-permute-start.3 = (f32[6,1,72,128]{3,2,1,0:T(8,128)S(1)}, f32[6,1,72,128]{3,2,1,0:T(8,128)S(1)}, u32[]{:S(2)}, u32[]{:S(2)}) collective-permute-start(f32[6,1,72,128]{3,2,1,0:T(8,128)S(1)} %maximum_bitcast_fusion.1), channel_id=1, source_target_pairs={{0,63},{1,0},{2,1},{3,2},{4,3},{5,4},{6,5},{7,6},{8,7},{9,8},{10,9... | collective-permute-start | bytes 663560 | tf_op jit(solution)/shard_map/ppermute | solution.py:21
  27.3 0.0 copy-start.11
  27.4 0.0 copy-start.12
  27.4 3.1 %collective-permute-start.2 = (f32[6,1,72,128]{3,2,1,0:T(8,128)S(1)}, f32[6,1,72,128]{3,2,1,0:T(8,128)S(1)}, u32[]{:S(2)}, u32[]{:S(2)}) collective-permute-start(f32[6,1,72,128]{3,2,1,0:T(8,128)S(1)} %maximum_bitcast_fusion), channel_id=1, source_target_pairs={{0,1},{1,2},{2,3},{3,4},{4,5},{5,6},{6,7},{7,8},{8,9},{9,10},{10,1... | collective-permute-start | bytes 663560 | tf_op jit(solution)/shard_map/ppermute | solution.py:21
  30.5 0.0 copy-done.12
  30.5 0.0 copy-start.4
  30.5 0.0 copy-start.5
  30.5 0.1 copy.42.w_out
  30.6 0.0 copy-done.11
  30.6 0.0 copy-start.1
  30.6 0.0 copy-start.9
  30.7 0.1 copy.41.w_tensor
  30.8 0.0 copy-start.3
  31.4 0.0 copy-done.1
  31.4 0.0 copy-start.8
  31.4 0.1 slice_reduce_fusion
  31.6 0.6 collective-permute-done.3.north
  32.1 2.4 %collective-permute-done.2.south = f32[6,1,72,128]{3,2,1,0:T(8,128)S(1)} collective-permute-done((f32[6,1,72,128]{3,2,1,0:T(8,128)S(1)}, f32[6,1,72,128]{3,2,1,0:T(8,128)S(1)}, u32[]{:S(2)}, u32[]{:S(2)}) %collective-permute-start.2) | collective-permute-done | bytes 221216 | tf_op jit(solution)/shard_map/ppermute | solution.py:21
  34.5 0.0 copy-done.4
  34.5 0.0 copy-done.5
  34.5 0.0 copy-done.9
  34.5 0.0 copy-done.3
  34.5 0.0 copy-done.8
  34.5 10.8 %shard_map.141 = (f32[4,4,128]{2,1,0:T(4,128)}, f32[3,6,128]{2,1,0:T(8,128)S(1)}, f32[3,6,128]{2,1,0:T(8,128)S(1)}, f32[4,3,6,128]{3,2,1,0:T(8,128)S(1)}) custom-call(s32[1,32]{1,0:T(1,128)S(1)} %bitcast.35, s32[1,1]{1,0:T(1,128)S(6)} %copy.59.live, s32[1,1,32,128]{3,2,1,0:T(8,128)S(1)} %copy-done.1, s32[1,1,32,128]{3,2,1,0:T(8,128)S(1)} %copy-done.3, ...), custom_call_target="tpu_custom_call" | custom-call | tf_op jit(solution)/shard_map/pallas_call | solution.py:352
  45.4 5.3 %collective-permute-start.4 = (f32[3,6,128]{2,1,0:T(8,128)S(1)}, f32[3,6,128]{2,1,0:T(8,128)S(1)}, u32[]{:S(2)}, u32[]{:S(2)}) collective-permute-start(f32[3,6,128]{2,1,0:T(8,128)S(1)} %get-tuple-element.60), channel_id=1, source_target_pairs={{0,704},{64,0},{128,64},{192,128},{256,192},{320,256},{384,320},{4... | collective-permute-start | bytes 27656 | tf_op jit(solution)/shard_map/ppermute | solution.py:21
  50.7 1.9 %collective-permute-start.5 = (f32[3,6,128]{2,1,0:T(8,128)S(1)}, f32[3,6,128]{2,1,0:T(8,128)S(1)}, u32[]{:S(2)}, u32[]{:S(2)}) collective-permute-start(f32[3,6,128]{2,1,0:T(8,128)S(1)} %get-tuple-element.61), channel_id=1, source_target_pairs={{0,64},{64,128},{128,192},{192,256},{256,320},{320,384},{384,448},... | collective-permute-start | bytes 27656 | tf_op jit(solution)/shard_map/ppermute | solution.py:21
  52.6 0.0 collective-permute-done.4
  52.6 3.7 %collective-permute-done.5 = f32[3,6,128]{2,1,0:T(8,128)S(1)} collective-permute-done((f32[3,6,128]{2,1,0:T(8,128)S(1)}, f32[3,6,128]{2,1,0:T(8,128)S(1)}, u32[]{:S(2)}, u32[]{:S(2)}) %collective-permute-start.5) | collective-permute-done | bytes 9248 | tf_op jit(solution)/shard_map/ppermute | solution.py:21
  56.4 11.0 %collective-permute-start.6 = (f32[4,3,128]{2,0,1:T(4,128)S(1)}, f32[4,3,128]{2,0,1:T(4,128)S(1)}, u32[]{:S(2)}, u32[]{:S(2)}) collective-permute-start(f32[4,3,128]{2,0,1:T(4,128)S(1)} %bitcast.38), channel_id=1, source_target_pairs={{0,63},{1,0},{2,1},{3,2},{4,3},{5,4},{6,5},{7,6},{8,7},{9,8},{10,9... | collective-permute-start | bytes 18440 | tf_op jit(solution)/shard_map/ppermute | solution.py:21
  67.4 1.9 %collective-permute-start.7 = (f32[4,3,128]{2,0,1:T(4,128)S(1)}, f32[4,3,128]{2,0,1:T(4,128)S(1)}, u32[]{:S(2)}, u32[]{:S(2)}) collective-permute-start(f32[4,3,128]{2,0,1:T(4,128)S(1)} %bitcast.37), channel_id=1, source_target_pairs={{0,1},{1,2},{2,3},{3,4},{4,5},{5,6},{6,7},{7,8},{8,9},{9,10},{10,1... | collective-permute-start | bytes 18440 | tf_op jit(solution)/shard_map/ppermute | solution.py:21
  69.4 0.0 collective-permute-done.6
  69.4 1.1 %collective-permute-done.7 = f32[4,3,128]{2,0,1:T(4,128)S(1)} collective-permute-done((f32[4,3,128]{2,0,1:T(4,128)S(1)}, f32[4,3,128]{2,0,1:T(4,128)S(1)}, u32[]{:S(2)}, u32[]{:S(2)}) %collective-permute-start.7) | collective-permute-done | bytes 6176 | tf_op jit(solution)/shard_map/ppermute | solution.py:21
  70.6 0.0 copy-start.10
  70.6 0.6 copy-done.10
  (16 shorter events, 0.3 us)
Async XLA Ops:
  0.6 1.0 %copy-start = (f32[4,4,64,128]{3,2,1,0:T(8,128)S(1)}, f32[4,4,64,128]{3,2,1,0:T(8,128)}, u32[]{:S(2)}) copy-start(f32[4,4,64,128]{3,2,1,0:T(8,128)} %feat.1) | copy-start | bytes 1572868
  1.7 0.7 %copy-start.2 = (f32[4,4,3,128]{3,1,2,0:T(4,128)S(1)}, f32[4,4,3,128]{3,1,2,0:T(4,128)}, u32[]{:S(2)}) copy-start(f32[4,4,3,128]{3,1,2,0:T(4,128)} %param.22) | copy-start | bytes 73732
  2.4 0.7 %copy-start.6 = (bf16[64,64]{1,0:T(8,128)(2,1)S(1)}, bf16[64,64]{1,0:T(8,128)(2,1)}, u32[]{:S(2)}) copy-start(bf16[64,64]{1,0:T(8,128)(2,1)} %w_center.1) | copy-start | bytes 24580
  3.1 0.7 %copy-start.7 = (bf16[64,64]{1,0:T(8,128)(2,1)S(1)}, bf16[64,64]{1,0:T(8,128)(2,1)}, u32[]{:S(2)}) copy-start(bf16[64,64]{1,0:T(8,128)(2,1)} %w_neigh.1) | copy-start | bytes 24580
  4.3 18.7 %collective-permute-start = (f32[1,4,72,128]{3,2,1,0:T(8,128)S(1)}, f32[1,4,72,128]{3,2,1,0:T(8,128)S(1)}, u32[]{:S(2)}, u32[]{:S(2)}) collective-permute-start(f32[1,4,72,128]{3,2,1,0:T(8,128)S(1)} %get-tuple-element.67), channel_id=1, source_target_pairs={{0,64},{64,128},{128,192},{192,256},{256,320},{320,384},{384,448},... | collective-permute-start | bytes 442376 | tf_op jit(solution)/shard_map/ppermute | solution.py:21
  9.1 14.7 %collective-permute-start.1 = (f32[1,4,72,128]{3,2,1,0:T(8,128)S(1)}, f32[1,4,72,128]{3,2,1,0:T(8,128)S(1)}, u32[]{:S(2)}, u32[]{:S(2)}) collective-permute-start(f32[1,4,72,128]{3,2,1,0:T(8,128)S(1)} %get-tuple-element.66), channel_id=1, source_target_pairs={{0,704},{64,0},{128,64},{192,128},{256,192},{320,256},{384,320},{4... | collective-permute-start | bytes 442376 | tf_op jit(solution)/shard_map/ppermute | solution.py:21
  23.9 8.2 %collective-permute-start.3 = (f32[6,1,72,128]{3,2,1,0:T(8,128)S(1)}, f32[6,1,72,128]{3,2,1,0:T(8,128)S(1)}, u32[]{:S(2)}, u32[]{:S(2)}) collective-permute-start(f32[6,1,72,128]{3,2,1,0:T(8,128)S(1)} %maximum_bitcast_fusion.1), channel_id=1, source_target_pairs={{0,63},{1,0},{2,1},{3,2},{4,3},{5,4},{6,5},{7,6},{8,7},{9,8},{10,9... | collective-permute-start | bytes 663560 | tf_op jit(solution)/shard_map/ppermute | solution.py:21
  27.3 3.3 %copy-start.11 = (bf16[64,16]{0,1:T(8,128)(2,1)S(1)}, bf16[64,16]{0,1:T(8,128)(2,1)}, u32[]{:S(2)}) copy-start(bf16[64,16]{0,1:T(8,128)(2,1)} %param.30) | copy-start | bytes 6148
  27.4 3.1 %copy-start.12 = (f32[64]{0:T(128)S(1)}, f32[64]{0:T(128)}, u32[]{:S(2)}) copy-start(f32[64]{0:T(128)} %param.33) | copy-start | bytes 772
  27.4 7.1 %collective-permute-start.2 = (f32[6,1,72,128]{3,2,1,0:T(8,128)S(1)}, f32[6,1,72,128]{3,2,1,0:T(8,128)S(1)}, u32[]{:S(2)}, u32[]{:S(2)}) collective-permute-start(f32[6,1,72,128]{3,2,1,0:T(8,128)S(1)} %maximum_bitcast_fusion), channel_id=1, source_target_pairs={{0,1},{1,2},{2,3},{3,4},{4,5},{5,6},{6,7},{7,8},{8,9},{9,10},{10,1... | collective-permute-start | bytes 663560 | tf_op jit(solution)/shard_map/ppermute | solution.py:21
  30.5 4.0 %copy-start.4 = (bf16[64,64]{1,0:T(8,128)(2,1)S(1)}, bf16[64,64]{1,0:T(8,128)(2,1)}, u32[]{:S(2)}) copy-start(bf16[64,64]{1,0:T(8,128)(2,1)} %w_latent.1) | copy-start | bytes 24580
  30.5 4.0 %copy-start.5 = (bf16[64,64]{1,0:T(8,128)(2,1)S(1)}, bf16[64,64]{1,0:T(8,128)(2,1)}, u32[]{:S(2)}) copy-start(bf16[64,64]{1,0:T(8,128)(2,1)} %w_mix.1) | copy-start | bytes 24580
  30.6 0.8 %copy-start.1 = (s32[1,1,32,128]{3,2,1,0:T(8,128)S(1)}, s32[1,1,32,128]{3,2,1,0:T(8,128)}, u32[]{:S(2)}) copy-start(s32[1,1,32,128]{3,2,1,0:T(8,128)} %centers.1) | copy-start | bytes 49156
  30.6 3.9 %copy-start.9 = (bf16[16,64]{1,0:T(8,128)(2,1)S(1)}, bf16[16,64]{1,0:T(8,128)(2,1)}, u32[]{:S(2)}) copy-start(bf16[16,64]{1,0:T(8,128)(2,1)} %w_env.1) | copy-start | bytes 6148
  30.8 3.8 %copy-start.3 = (s32[1,1,32,128]{3,2,1,0:T(8,128)S(1)}, s32[1,1,32,128]{3,2,1,0:T(8,128)}, u32[]{:S(2)}) copy-start(s32[1,1,32,128]{3,2,1,0:T(8,128)} %neighbours.1) | copy-start | bytes 49156
  31.4 3.1 %copy-start.8 = (f32[8,64]{1,0:T(8,128)S(1)}, f32[8,64]{1,0:T(8,128)}, u32[]{:S(2)}) copy-start(f32[8,64]{1,0:T(8,128)} %w_radial.1) | copy-start | bytes 6148
  45.4 7.3 %collective-permute-start.4 = (f32[3,6,128]{2,1,0:T(8,128)S(1)}, f32[3,6,128]{2,1,0:T(8,128)S(1)}, u32[]{:S(2)}, u32[]{:S(2)}) collective-permute-start(f32[3,6,128]{2,1,0:T(8,128)S(1)} %get-tuple-element.60), channel_id=1, source_target_pairs={{0,704},{64,0},{128,64},{192,128},{256,192},{320,256},{384,320},{4... | collective-permute-start | bytes 27656 | tf_op jit(solution)/shard_map/ppermute | solution.py:21
  50.7 5.7 %collective-permute-start.5 = (f32[3,6,128]{2,1,0:T(8,128)S(1)}, f32[3,6,128]{2,1,0:T(8,128)S(1)}, u32[]{:S(2)}, u32[]{:S(2)}) collective-permute-start(f32[3,6,128]{2,1,0:T(8,128)S(1)} %get-tuple-element.61), channel_id=1, source_target_pairs={{0,64},{64,128},{128,192},{192,256},{256,320},{320,384},{384,448},... | collective-permute-start | bytes 27656 | tf_op jit(solution)/shard_map/ppermute | solution.py:21
  56.4 13.0 %collective-permute-start.6 = (f32[4,3,128]{2,0,1:T(4,128)S(1)}, f32[4,3,128]{2,0,1:T(4,128)S(1)}, u32[]{:S(2)}, u32[]{:S(2)}) collective-permute-start(f32[4,3,128]{2,0,1:T(4,128)S(1)} %bitcast.38), channel_id=1, source_target_pairs={{0,63},{1,0},{2,1},{3,2},{4,3},{5,4},{6,5},{7,6},{8,7},{9,8},{10,9... | collective-permute-start | bytes 18440 | tf_op jit(solution)/shard_map/ppermute | solution.py:21
  67.4 3.1 %collective-permute-start.7 = (f32[4,3,128]{2,0,1:T(4,128)S(1)}, f32[4,3,128]{2,0,1:T(4,128)S(1)}, u32[]{:S(2)}, u32[]{:S(2)}) collective-permute-start(f32[4,3,128]{2,0,1:T(4,128)S(1)} %bitcast.37), channel_id=1, source_target_pairs={{0,1},{1,2},{2,3},{3,4},{4,5},{5,6},{6,7},{7,8},{8,9},{9,10},{10,1... | collective-permute-start | bytes 18440 | tf_op jit(solution)/shard_map/ppermute | solution.py:21
  70.6 0.6 copy-start.10

commit v3 on v2

--- a/solution.py
+++ b/solution.py
@@ -12,13 +12,17 @@
 GROUP = 32
 F32 = jnp.float32
 BF16 = jnp.bfloat16
+SMALL = pltpu.CompilerParams(vmem_limit_bytes=8 * 1024 * 1024)
 SIN_TERMS = (3.14159265358979, -5.16771278004997, 2.55016403987735, -0.599264529320792, 0.0821458866111282, -0.00737043094571435)
 COS_TERMS = (1.0, -4.93480220054468, 4.05871212641677, -1.33526276885459, 0.235330630358893, -0.0258068913900141, 0.00192957430940392)
 
 
-def shifted(array, axis, by):
+def swapped(array, axis, far):
     length = lax.axis_size(axis)
-    return lax.ppermute(array, axis, [(i, (i + by) % length) for i in range(length)])
+    pairs = []
+    for low in range(far, length + far, 2):
+        pairs += [(low % length, (low + 1) % length), ((low + 1) % length, low % length)]
+    return lax.ppermute(array, axis, pairs)
 
 
 def split(array):
@@ -38,9 +42,9 @@
     return jnp.dot(left, right, preferred_element_type=F32)
 
 
-def tables_kernel(feat, coord, w_center, w_neigh, table_c, packed):
+def tables_kernel(feat, coord, w_both, table_c, packed, send_far, send_near):
     inner_x, inner_y, lat, slots = feat.shape
-    both = 0.5 * jnp.concatenate([w_center[...].astype(F32), w_neigh[...].astype(F32)], 1)
+    both = 0.5 * w_both[...].astype(F32)
     both = jnp.concatenate([both, both], 0).T.astype(BF16)
     pad = jnp.zeros((ROWS - lat - 3, slots), F32)
     for x in range(inner_x):
@@ -52,18 +56,43 @@
             table_c[x * inner_y + y] = piece[:lat]
             packed[x, y, :lat] = piece[lat:]
             packed[x, y, lat:] = jnp.concatenate([coord[x, m, y : y + 1] for m in range(3)] + [pad], 0)
+    odd = lax.axis_index("bx") % 2
+    last = inner_x - 1
+    send_far[...] = packed[last * odd]
+    send_near[...] = packed[last * (1 - odd)]
 
 
 def tables(features, coords, w_center, w_neigh):
     inner_x, inner_y, lat, slots = features.shape
+    side = jax.ShapeDtypeStruct((inner_y, ROWS, slots), F32)
     return pl.pallas_call(
         tables_kernel,
         out_shape=(
             jax.ShapeDtypeStruct((inner_x * inner_y, lat, slots), F32),
             jax.ShapeDtypeStruct((inner_x, inner_y, ROWS, slots), F32),
+            side,
+            side,
         ),
-        compiler_params=pltpu.CompilerParams(vmem_limit_bytes=16 * 1024 * 1024),
-    )(features, coords, w_center, w_neigh)
+        compiler_params=SMALL,
+    )(features, coords, jnp.concatenate([w_center, w_neigh], 1))
+
+
+def sides_kernel(packed, from_far, from_near, send_far, send_near):
+    inner_x, inner_y = packed.shape[:2]
+    odd_x = lax.axis_index("bx") % 2
+    odd_y = lax.axis_index("by") % 2
+    for send, odd in ((send_far, odd_y), (send_near, 1 - odd_y)):
+        row = (inner_y - 1) * odd
+        send[(inner_x + 1) * odd_x] = from_far[row]
+        send[(inner_x + 1) * (1 - odd_x)] = from_near[row]
+        for x in range(inner_x):
+            send[x + 1] = packed[x, row]
+
+
+def sides(packed, from_far, from_near):
+    inner_x, _, rows, slots = packed.shape
+    send = jax.ShapeDtypeStruct((inner_x + 2, rows, slots), F32)
+    return pl.pallas_call(sides_kernel, out_shape=(send, send), compiler_params=SMALL)(packed, from_far, from_near)
 
 
 def sine_cosine(turns):
@@ -98,10 +127,10 @@
     neighbours,
     table_c,
     packed,
-    west,
-    east,
-    south,
-    north,
+    far_x,
+    near_x,
+    far_y,
+    near_y,
     w_radial,
     w_latent,
     w_tensor,
@@ -109,8 +138,8 @@
     w_env,
     w_out,
     energies,
-    push_west,
-    push_east,
+    push_far,
+    push_near,
     push_inner,
     table_n,
     gamma,
@@ -129,19 +158,21 @@
     ch = w_tensor.shape[1]
     nb = w_radial.shape[0]
     width = GROUP * slots
+    odd_x = lax.axis_index("bx") % 2
+    odd_y = lax.axis_index("by") % 2
+    far_x_at = (inner_x + 1) * odd_x
+    near_x_at = (inner_x + 1) * (1 - odd_x)
+    far_y_at = (inner_y + 1) * odd_y
+    near_y_at = (inner_y + 1) * (1 - odd_y)
+    for y in range(inner_y):
+        for x in range(inner_x):
+            table_n[(x + 1) * wide_y + y + 1] = packed[x, y]
+        table_n[far_x_at * wide_y + y + 1] = far_x[y]
+        table_n[near_x_at * wide_y + y + 1] = near_x[y]
     for x in range(inner_x + 2):
-        for y in range(wide_y):
-            if y == 0:
-                source = south[x, 0]
-            elif y == inner_y + 1:
-                source = north[x, 0]
-            elif x == 0:
-                source = west[0, y - 1]
-            elif x == inner_x + 1:
-                source = east[0, y - 1]
-            else:
-                source = packed[x - 1, y - 1]
-            table_n[x * wide_y + y] = source
+        table_n[x * wide_y + far_y_at] = far_y[x]
+        table_n[x * wide_y + near_y_at] = near_y[x]
+
     gamma[...] = jnp.zeros_like(gamma)
     g_gamma[...] = jnp.zeros_like(g_gamma)
     push[...] = jnp.zeros_like(push)
@@ -323,22 +354,70 @@
 
     lax.fori_loop(0, groups, backward, 0)
 
-    for x in range(inner_x + 2):
-        for y in range(wide_y):
-            both = push[x * wide_y + y]
-            total = both[0:4] + both[4:8]
+    def total(cell):
+        both = push[cell]
+        return both[0:4] + both[4:8]
+
+    for y in range(wide_y):
+        for target, x in ((push_far, far_x_at), (push_near, near_x_at)):
+            sums = total(x * wide_y + y)
             for m in range(3):
-                if x == 0:
-                    push_west[m, y : y + 1] = total[m : m + 1]
-                elif x == inner_x + 1:
-                    push_east[m, y : y + 1] = total[m : m + 1]
-                else:
-                    push_inner[x - 1, m, y : y + 1] = total[m : m + 1]
-            if 1 <= x <= inner_x and 1 <= y <= inner_y:
-                energies[x - 1, y - 1 : y] = total[3:4]
-
-
-def brick(centers, neighbours, live_blocks, table_c, packed, west, east, south, north, *weights):
+                target[m, y : y + 1] = sums[m : m + 1]
+        for x in range(inner_x):
+            sums = total((x + 1) * wide_y + y)
+            for m in range(3):
+                push_inner[x, m, y : y + 1] = sums[m : m + 1]
+            if 1 <= y <= inner_y:
+                energies[x, y - 1 : y] = sums[3:4]
+
+
+def turned_kernel(inner, from_far, from_near, send_far, send_near, kept, work):
+    inner_x, _, wide_y, _ = inner.shape
+    odd_x = lax.axis_index("bx") % 2
+    odd_y = lax.axis_index("by") % 2
+    work[...] = inner[...]
+    work[(inner_x - 1) * odd_x] += from_far[...]
+    work[(inner_x - 1) * (1 - odd_x)] += from_near[...]
+    for x in range(inner_x):
+        for m in range(3):
+            rows = work[x, m]
+            low, high = rows[:1], rows[wide_y - 1 :]
+            send_far[x, m : m + 1] = jnp.where(odd_y == 1, high, low)
+            send_near[x, m : m + 1] = jnp.where(odd_y == 1, low, high)
+            kept[x, m] = rows[1 : wide_y - 1]
+
+
+def turned(inner, from_far, from_near):
+    inner_x, _, wide_y, slots = inner.shape
+    send = jax.ShapeDtypeStruct((inner_x, 3, slots), F32)
+    return pl.pallas_call(
+        turned_kernel,
+        out_shape=(send, send, jax.ShapeDtypeStruct((inner_x, 3, wide_y - 2, slots), F32)),
+        scratch_shapes=[pltpu.VMEM(inner.shape, F32)],
+        compiler_params=SMALL,
+    )(inner, from_far, from_near)
+
+
+def final_kernel(kept, from_far, from_near, forces):
+    inner_x, _, inner_y, slots = kept.shape
+    odd_y = lax.axis_index("by") % 2
+    rows = lax.broadcasted_iota(jnp.int32, (inner_y, slots), 0)
+    far_at = (inner_y - 1) * odd_y
+    near_at = (inner_y - 1) * (1 - odd_y)
+    for x in range(inner_x):
+        for m in range(3):
+            far = jnp.where(rows == far_at, from_far[x, m : m + 1], 0.0)
+            near = jnp.where(rows == near_at, from_near[x, m : m + 1], 0.0)
+            forces[x, m] = kept[x, m] + far + near
+
+
+def final(kept, from_far, from_near):
+    return pl.pallas_call(
+        final_kernel, out_shape=jax.ShapeDtypeStruct(kept.shape, F32), compiler_params=SMALL
+    )(kept, from_far, from_near)
+
+
+def brick(centers, neighbours, live_blocks, table_c, packed, far_x, near_x, far_y, near_y, *weights):
     inner_x, inner_y, rows, slots = packed.shape
     blocks = centers.shape[2]
     lat = table_c.shape[1]
@@ -372,7 +451,7 @@
             pltpu.VMEM((groups, 16, width), F32),
         ],
         compiler_params=pltpu.CompilerParams(vmem_limit_bytes=40 * 1024 * 1024),
-    )(centers[0, :, :, 0], live_blocks, centers, neighbours, table_c, packed, west, east, south, north, *weights)
+    )(centers[0, :, :, 0], live_blocks, centers, neighbours, table_c, packed, far_x, near_x, far_y, near_y, *weights)
 
 
 def body(
@@ -390,26 +469,23 @@
     w_env,
     w_out,
 ):
-    table_c, packed = tables(features, jnp.swapaxes(coords, 1, 2), w_center, w_neigh)
+    table_c, packed, send_far, send_near = tables(features, jnp.swapaxes(coords, 1, 2), w_center, w_neigh)
     inner_x, inner_y = packed.shape[:2]
-    west = shifted(packed[inner_x - 1 :], "bx", 1)
-    east = shifted(packed[:1], "bx", -1)
-    top = jnp.concatenate([west[:, inner_y - 1], packed[:, inner_y - 1], east[:, inner_y - 1]], 0)
-    bottom = jnp.concatenate([west[:, 0], packed[:, 0], east[:, 0]], 0)
-    south = shifted(top[:, None], "by", 1)
-    north = shifted(bottom[:, None], "by", -1)
+    far_x = swapped(send_far, "bx", 1)
+    near_x = swapped(send_near, "bx", 0)
+    send_far, send_near = sides(packed, far_x, near_x)
+    far_y = swapped(send_far, "by", 1)
+    near_y = swapped(send_near, "by", 0)
     weights = (w_radial, w_latent, w_tensor, w_mix, w_env, w_out[:, None])
-    energies, push_west, push_east, inner = brick(
-        centers, neighbours, live_blocks, table_c, packed, west, east, south, north, *weights
+    energies, push_far, push_near, inner = brick(
+        centers, neighbours, live_blocks, table_c, packed, far_x, near_x, far_y, near_y, *weights
     )
-    from_east = shifted(push_west, "bx", -1)
-    from_west = shifted(push_east, "bx", 1)
-    inner = inner.at[inner_x - 1].add(from_east).at[0].add(from_west)
-    from_north = shifted(inner[:, :, 0], "by", -1)
-    from_south = shifted(inner[:, :, inner_y + 1], "by", 1)
-    forces = inner[:, :, 1 : inner_y + 1]
-    forces = forces.at[:, :, inner_y - 1].add(from_north).at[:, :, 0].add(from_south)
-    forces = jnp.swapaxes(forces, 1, 2)
+    from_far = swapped(push_far, "bx", 1)
+    from_near = swapped(push_near, "bx", 0)
+    send_far, send_near, kept = turned(inner, from_far, from_near)
+    from_far = swapped(send_far, "by", 1)
+    from_near = swapped(send_near, "by", 0)
+    forces = jnp.swapaxes(final(kept, from_far, from_near), 1, 2)
     return (energies, forces)
 
 

time: 71.9 us -> 64.1 us (0.89)
  starting transfers between devices: 43.8 us -> 39.8 us
  waiting for transfers between devices: 10.2 us -> 7.69 us
  local copies, waits for them, and re-layouts: 4.34 us -> 1.9 us
  other arithmetic: 0.07 us -> 0.82 us
    ppermute x8, starting transfers between devices: 43.8 us -> 39.8 us  [swapped(): return lax.ppermute(array, axis, pairs)]
    ppermute x8, waiting for transfers between devices: 10.2 us -> 7.69 us  [swapped(): return lax.ppermute(array, axis, pairs)]
    unnamed x27 -> x21, local copies, waits for them, and re-layouts: 3.95 us -> 1.69 us
    concatenate x0 -> x1, other arithmetic: none -> 0.82 us  [tables(): jnp.concatenate([w_center, w_neigh], 1)]
  transfers between devices with their start and end apart: 8 -> 8, of which waited for: 6 -> 5; matrix products, arithmetic and copies ran while one was open for 1% -> 0% of each run, Pallas kernels for 0% -> 0%
where the time goes in v3:
time: 64.1 us; the launch traced here: 63.6 us
  starting transfers between devices  39.8 us (62%)
  Pallas kernels  11.9 us (19%)
  waiting for transfers between devices  7.69 us (12%)
  local copies, waits for them, and re-layouts  1.9 us (3%)
  between operations  1.5 us (2%)
  other arithmetic  0.82 us (1%)
    ppermute x8, starting transfers between devices, swapped(): return lax.ppermute(array, axis, pairs)  39.8 us
    pallas_call x1, Pallas kernels, brick(): pl.pallas_call(brick_kernel, in_specs=[smem, smem] + [vmem] * 14, out_spe...  10.8 us
    ppermute x8, waiting for transfers between devices, swapped(): return lax.ppermute(array, axis, pairs)  7.69 us
    unnamed x21, local copies, waits for them, and re-layouts  1.69 us
  transfers between devices with their start and end apart: 8, of which 5 were waited for; matrix products, arithmetic and copies ran while one was open for 0% of the time, Pallas kernels for 0%

profile of v3, /device:TPU:1, one launch (start us, length us, event | category | flops | bytes accessed | tf_op | source)
XLA Modules:
  0.0 63.6 jit_solution(3308129939470126791)
XLA Ops:
  0.6 0.0 copy-start.2
  0.6 0.8 %pad_maximum_fusion.w_both = bf16[64,128]{1,0:T(8,128)(2,1)S(1)} fusion(bf16[64,64]{1,0:T(8,128)(2,1)} %param.19, bf16[64,64]{1,0:T(8,128)(2,1)} %param.18), kind=kLoop, calls=%fused_computation | loop fusion | flops 32768 | bytes 32768 | tf_op jit(solution)/shard_map/concatenate | solution.py:77
  1.5 0.0 copy-done.2
  1.5 0.0 copy-start
  1.5 1.0 %copy-done = f32[4,4,64,128]{3,2,1,0:T(8,128)S(1)} copy-done((f32[4,4,64,128]{3,2,1,0:T(8,128)S(1)}, f32[4,4,64,128]{3,2,1,0:T(8,128)}, u32[]{:S(2)}) %copy-start) | copy-done | bytes 524312
  2.5 0.4 shard_map.140
  2.9 15.1 %collective-permute-start = (f32[4,72,128]{2,1,0:T(8,128)S(1)}, f32[4,72,128]{2,1,0:T(8,128)S(1)}, u32[]{:S(2)}, u32[]{:S(2)}) collective-permute-start(f32[4,72,128]{2,1,0:T(8,128)S(1)} %get-tuple-element.17), channel_id=1, source_target_pairs={{64,128},{128,64},{192,256},{256,192},{320,384},{384,320},{448,512... | collective-permute-start | bytes 442376 | tf_op jit(solution)/shard_map/ppermute | solution.py:25
  18.0 1.9 %collective-permute-start.1 = (f32[4,72,128]{2,1,0:T(8,128)S(1)}, f32[4,72,128]{2,1,0:T(8,128)S(1)}, u32[]{:S(2)}, u32[]{:S(2)}) collective-permute-start(f32[4,72,128]{2,1,0:T(8,128)S(1)} %get-tuple-element.18), channel_id=1, source_target_pairs={{0,64},{64,0},{128,192},{192,128},{256,320},{320,256},{384,448},{4... | collective-permute-start | bytes 442376 | tf_op jit(solution)/shard_map/ppermute | solution.py:25
  20.0 1.6 %collective-permute-done.from_far.far_x = f32[4,72,128]{2,1,0:T(8,128)S(1)} collective-permute-done((f32[4,72,128]{2,1,0:T(8,128)S(1)}, f32[4,72,128]{2,1,0:T(8,128)S(1)}, u32[]{:S(2)}, u32[]{:S(2)}) %collective-permute-start) | collective-permute-done | bytes 147488 | tf_op jit(solution)/shard_map/ppermute | solution.py:25
  21.6 2.7 %collective-permute-done.1.from_near.near_x = f32[4,72,128]{2,1,0:T(8,128)S(1)} collective-permute-done((f32[4,72,128]{2,1,0:T(8,128)S(1)}, f32[4,72,128]{2,1,0:T(8,128)S(1)}, u32[]{:S(2)}, u32[]{:S(2)}) %collective-permute-start.1) | collective-permute-done | bytes 147488 | tf_op jit(solution)/shard_map/ppermute | solution.py:25
  24.3 0.0 copy-start.8
  24.4 5.0 %collective-permute-start.2 = (f32[6,72,128]{2,1,0:T(8,128)S(1)}, f32[6,72,128]{2,1,0:T(8,128)S(1)}, u32[]{:S(2)}, u32[]{:S(2)}) collective-permute-start(f32[6,72,128]{2,1,0:T(8,128)S(1)} %get-tuple-element.19), channel_id=1, source_target_pairs={{1,2},{2,1},{3,4},{4,3},{5,6},{6,5},{7,8},{8,7},{9,10},{10,9},{11,... | collective-permute-start | bytes 663560 | tf_op jit(solution)/shard_map/ppermute | solution.py:25
  29.3 0.0 copy-start.9
  29.3 4.7 %collective-permute-start.3 = (f32[6,72,128]{2,1,0:T(8,128)S(1)}, f32[6,72,128]{2,1,0:T(8,128)S(1)}, u32[]{:S(2)}, u32[]{:S(2)}) collective-permute-start(f32[6,72,128]{2,1,0:T(8,128)S(1)} %get-tuple-element.20), channel_id=1, source_target_pairs={{0,1},{1,0},{2,3},{3,2},{4,5},{5,4},{6,7},{7,6},{8,9},{9,8},{10,11... | collective-permute-start | bytes 663560 | tf_op jit(solution)/shard_map/ppermute | solution.py:25
  34.0 0.0 copy-done.9
  34.0 0.0 copy-start.4
  34.0 0.0 copy-start.5
  34.0 0.1 copy.18.w_out
  34.1 0.0 copy-done.8
  34.1 0.0 copy-start.1
  34.2 0.0 copy-start.7
  34.2 0.1 copy.17.w_tensor
  34.3 0.0 copy-start.3
  34.9 0.0 copy-done.1
  34.9 0.0 copy-start.6
  35.0 0.1 slice_reduce_fusion
  35.1 0.0 collective-permute-done.2.far_y
  35.1 0.0 collective-permute-done.3.near_y
  35.1 0.0 copy-done.4
  35.1 0.0 copy-done.5
  35.1 0.0 copy-done.7
  35.1 0.0 copy-done.3
  35.1 0.5 copy-done.6
  35.6 10.8 %shard_map.142 = (f32[4,4,128]{2,1,0:T(4,128)}, f32[3,6,128]{2,1,0:T(8,128)S(1)}, f32[3,6,128]{2,1,0:T(8,128)S(1)}, f32[4,3,6,128]{3,2,1,0:T(8,128)S(1)}) custom-call(s32[1,32]{1,0:T(1,128)S(1)} %bitcast.5, s32[1,1]{1,0:T(1,128)S(6)} %copy.19.live, s32[1,1,32,128]{3,2,1,0:T(8,128)S(1)} %copy-done.1, s32[1,1,32,128]{3,2,1,0:T(8,128)S(1)} %copy-done.3, ...), custom_call_target="tpu_custom_call" | custom-call | tf_op jit(solution)/shard_map/pallas_call | solution.py:431
  46.5 2.2 %collective-permute-start.4 = (f32[3,6,128]{2,1,0:T(8,128)S(1)}, f32[3,6,128]{2,1,0:T(8,128)S(1)}, u32[]{:S(2)}, u32[]{:S(2)}) collective-permute-start(f32[3,6,128]{2,1,0:T(8,128)S(1)} %get-tuple-element.23), channel_id=1, source_target_pairs={{64,128},{128,64},{192,256},{256,192},{320,384},{384,320},{448,512... | collective-permute-start | bytes 27656 | tf_op jit(solution)/shard_map/ppermute | solution.py:25
  48.7 1.9 %collective-permute-start.5 = (f32[3,6,128]{2,1,0:T(8,128)S(1)}, f32[3,6,128]{2,1,0:T(8,128)S(1)}, u32[]{:S(2)}, u32[]{:S(2)}) collective-permute-start(f32[3,6,128]{2,1,0:T(8,128)S(1)} %get-tuple-element.24), channel_id=1, source_target_pairs={{0,64},{64,0},{128,192},{192,128},{256,320},{320,256},{384,448},{4... | collective-permute-start | bytes 27656 | tf_op jit(solution)/shard_map/ppermute | solution.py:25
  50.6 1.5 %collective-permute-done.4.from_far = f32[3,6,128]{2,1,0:T(8,128)S(1)} collective-permute-done((f32[3,6,128]{2,1,0:T(8,128)S(1)}, f32[3,6,128]{2,1,0:T(8,128)S(1)}, u32[]{:S(2)}, u32[]{:S(2)}) %collective-permute-start.4) | collective-permute-done | bytes 9248 | tf_op jit(solution)/shard_map/ppermute | solution.py:25
  52.1 1.0 %collective-permute-done.5.from_near = f32[3,6,128]{2,1,0:T(8,128)S(1)} collective-permute-done((f32[3,6,128]{2,1,0:T(8,128)S(1)}, f32[3,6,128]{2,1,0:T(8,128)S(1)}, u32[]{:S(2)}, u32[]{:S(2)}) %collective-permute-start.5) | collective-permute-done | bytes 9248 | tf_op jit(solution)/shard_map/ppermute | solution.py:25
  53.2 2.1 %collective-permute-start.6 = (f32[4,3,128]{2,1,0:T(4,128)S(1)}, f32[4,3,128]{2,1,0:T(4,128)S(1)}, u32[]{:S(2)}, u32[]{:S(2)}) collective-permute-start(f32[4,3,128]{2,1,0:T(4,128)S(1)} %get-tuple-element.26), channel_id=1, source_target_pairs={{1,2},{2,1},{3,4},{4,3},{5,6},{6,5},{7,8},{8,7},{9,10},{10,9},{11,... | collective-permute-start | bytes 18440 | tf_op jit(solution)/shard_map/ppermute | solution.py:25
  55.3 6.9 %collective-permute-start.7 = (f32[4,3,128]{2,1,0:T(4,128)S(1)}, f32[4,3,128]{2,1,0:T(4,128)S(1)}, u32[]{:S(2)}, u32[]{:S(2)}) collective-permute-start(f32[4,3,128]{2,1,0:T(4,128)S(1)} %get-tuple-element.27), channel_id=1, source_target_pairs={{0,1},{1,0},{2,3},{3,2},{4,5},{5,4},{6,7},{7,6},{8,9},{9,8},{10,11... | collective-permute-start | bytes 18440 | tf_op jit(solution)/shard_map/ppermute | solution.py:25
  62.2 0.0 collective-permute-done.6.from_far
  62.2 0.8 %collective-permute-done.7.from_near = f32[4,3,128]{2,1,0:T(4,128)S(1)} collective-permute-done((f32[4,3,128]{2,1,0:T(4,128)S(1)}, f32[4,3,128]{2,1,0:T(4,128)S(1)}, u32[]{:S(2)}, u32[]{:S(2)}) %collective-permute-start.7) | collective-permute-done | bytes 6176 | tf_op jit(solution)/shard_map/ppermute | solution.py:25
  63.0 0.6 shard_map.144
  (2 shorter events, 0.1 us)
Async XLA Ops:
  0.6 0.8 %copy-start.2 = (f32[4,4,3,128]{3,1,2,0:T(4,128)S(1)}, f32[4,4,3,128]{3,1,2,0:T(4,128)}, u32[]{:S(2)}) copy-start(f32[4,4,3,128]{3,1,2,0:T(4,128)} %param.14) | copy-start | bytes 73732
  1.5 1.0 %copy-start = (f32[4,4,64,128]{3,2,1,0:T(8,128)S(1)}, f32[4,4,64,128]{3,2,1,0:T(8,128)}, u32[]{:S(2)}) copy-start(f32[4,4,64,128]{3,2,1,0:T(8,128)} %feat.1) | copy-start | bytes 1572868
  2.9 18.7 %collective-permute-start = (f32[4,72,128]{2,1,0:T(8,128)S(1)}, f32[4,72,128]{2,1,0:T(8,128)S(1)}, u32[]{:S(2)}, u32[]{:S(2)}) collective-permute-start(f32[4,72,128]{2,1,0:T(8,128)S(1)} %get-tuple-element.17), channel_id=1, source_target_pairs={{64,128},{128,64},{192,256},{256,192},{320,384},{384,320},{448,512... | collective-permute-start | bytes 442376 | tf_op jit(solution)/shard_map/ppermute | solution.py:25
  18.0 6.3 %collective-permute-start.1 = (f32[4,72,128]{2,1,0:T(8,128)S(1)}, f32[4,72,128]{2,1,0:T(8,128)S(1)}, u32[]{:S(2)}, u32[]{:S(2)}) collective-permute-start(f32[4,72,128]{2,1,0:T(8,128)S(1)} %get-tuple-element.18), channel_id=1, source_target_pairs={{0,64},{64,0},{128,192},{192,128},{256,320},{320,256},{384,448},{4... | collective-permute-start | bytes 442376 | tf_op jit(solution)/shard_map/ppermute | solution.py:25
  24.3 9.8 %copy-start.8 = (bf16[64,16]{0,1:T(8,128)(2,1)S(1)}, bf16[64,16]{0,1:T(8,128)(2,1)}, u32[]{:S(2)}) copy-start(bf16[64,16]{0,1:T(8,128)(2,1)} %param.22) | copy-start | bytes 6148
  24.4 10.7 %collective-permute-start.2 = (f32[6,72,128]{2,1,0:T(8,128)S(1)}, f32[6,72,128]{2,1,0:T(8,128)S(1)}, u32[]{:S(2)}, u32[]{:S(2)}) collective-permute-start(f32[6,72,128]{2,1,0:T(8,128)S(1)} %get-tuple-element.19), channel_id=1, source_target_pairs={{1,2},{2,1},{3,4},{4,3},{5,6},{6,5},{7,8},{8,7},{9,10},{10,9},{11,... | collective-permute-start | bytes 663560 | tf_op jit(solution)/shard_map/ppermute | solution.py:25
  29.3 4.7 %copy-start.9 = (f32[64]{0:T(128)S(1)}, f32[64]{0:T(128)}, u32[]{:S(2)}) copy-start(f32[64]{0:T(128)} %param.25) | copy-start | bytes 772
  29.3 5.8 %collective-permute-start.3 = (f32[6,72,128]{2,1,0:T(8,128)S(1)}, f32[6,72,128]{2,1,0:T(8,128)S(1)}, u32[]{:S(2)}, u32[]{:S(2)}) collective-permute-start(f32[6,72,128]{2,1,0:T(8,128)S(1)} %get-tuple-element.20), channel_id=1, source_target_pairs={{0,1},{1,0},{2,3},{3,2},{4,5},{5,4},{6,7},{7,6},{8,9},{9,8},{10,11... | collective-permute-start | bytes 663560 | tf_op jit(solution)/shard_map/ppermute | solution.py:25
  34.0 1.1 %copy-start.4 = (bf16[64,64]{1,0:T(8,128)(2,1)S(1)}, bf16[64,64]{1,0:T(8,128)(2,1)}, u32[]{:S(2)}) copy-start(bf16[64,64]{1,0:T(8,128)(2,1)} %w_latent.1) | copy-start | bytes 24580
  34.0 1.1 %copy-start.5 = (bf16[64,64]{1,0:T(8,128)(2,1)S(1)}, bf16[64,64]{1,0:T(8,128)(2,1)}, u32[]{:S(2)}) copy-start(bf16[64,64]{1,0:T(8,128)(2,1)} %w_mix.1) | copy-start | bytes 24580
  34.1 0.8 %copy-start.1 = (s32[1,1,32,128]{3,2,1,0:T(8,128)S(1)}, s32[1,1,32,128]{3,2,1,0:T(8,128)}, u32[]{:S(2)}) copy-start(s32[1,1,32,128]{3,2,1,0:T(8,128)} %centers.1) | copy-start | bytes 49156
  34.2 1.0 %copy-start.7 = (bf16[16,64]{1,0:T(8,128)(2,1)S(1)}, bf16[16,64]{1,0:T(8,128)(2,1)}, u32[]{:S(2)}) copy-start(bf16[16,64]{1,0:T(8,128)(2,1)} %w_env.1) | copy-start | bytes 6148
  34.3 0.8 %copy-start.3 = (s32[1,1,32,128]{3,2,1,0:T(8,128)S(1)}, s32[1,1,32,128]{3,2,1,0:T(8,128)}, u32[]{:S(2)}) copy-start(s32[1,1,32,128]{3,2,1,0:T(8,128)} %neighbours.1) | copy-start | bytes 49156
  34.9 0.7 %copy-start.6 = (f32[8,64]{1,0:T(8,128)S(1)}, f32[8,64]{1,0:T(8,128)}, u32[]{:S(2)}) copy-start(f32[8,64]{1,0:T(8,128)} %w_radial.1) | copy-start | bytes 6148
  46.5 5.6 %collective-permute-start.4 = (f32[3,6,128]{2,1,0:T(8,128)S(1)}, f32[3,6,128]{2,1,0:T(8,128)S(1)}, u32[]{:S(2)}, u32[]{:S(2)}) collective-permute-start(f32[3,6,128]{2,1,0:T(8,128)S(1)} %get-tuple-element.23), channel_id=1, source_target_pairs={{64,128},{128,64},{192,256},{256,192},{320,384},{384,320},{448,512... | collective-permute-start | bytes 27656 | tf_op jit(solution)/shard_map/ppermute | solution.py:25
  48.7 4.4 %collective-permute-start.5 = (f32[3,6,128]{2,1,0:T(8,128)S(1)}, f32[3,6,128]{2,1,0:T(8,128)S(1)}, u32[]{:S(2)}, u32[]{:S(2)}) collective-permute-start(f32[3,6,128]{2,1,0:T(8,128)S(1)} %get-tuple-element.24), channel_id=1, source_target_pairs={{0,64},{64,0},{128,192},{192,128},{256,320},{320,256},{384,448},{4... | collective-permute-start | bytes 27656 | tf_op jit(solution)/shard_map/ppermute | solution.py:25
  53.2 9.0 %collective-permute-start.6 = (f32[4,3,128]{2,1,0:T(4,128)S(1)}, f32[4,3,128]{2,1,0:T(4,128)S(1)}, u32[]{:S(2)}, u32[]{:S(2)}) collective-permute-start(f32[4,3,128]{2,1,0:T(4,128)S(1)} %get-tuple-element.26), channel_id=1, source_target_pairs={{1,2},{2,1},{3,4},{4,3},{5,6},{6,5},{7,8},{8,7},{9,10},{10,9},{11,... | collective-permute-start | bytes 18440 | tf_op jit(solution)/shard_map/ppermute | solution.py:25
  55.3 7.7 %collective-permute-start.7 = (f32[4,3,128]{2,1,0:T(4,128)S(1)}, f32[4,3,128]{2,1,0:T(4,128)S(1)}, u32[]{:S(2)}, u32[]{:S(2)}) collective-permute-start(f32[4,3,128]{2,1,0:T(4,128)S(1)} %get-tuple-element.27), channel_id=1, source_target_pairs={{0,1},{1,0},{2,3},{3,2},{4,5},{5,4},{6,7},{7,6},{8,9},{9,8},{10,11... | collective-permute-start | bytes 18440 | tf_op jit(solution)/shard_map/ppermute | solution.py:25

commit v4 on v3

--- a/solution.py
+++ b/solution.py
@@ -10,6 +10,7 @@
 SOFTEN = 0.25
 ROWS = 72
 GROUP = 32
+HALO_X, HALO_Y, BACK_X, BACK_Y = 0, 0, 0, 0
 F32 = jnp.float32
 BF16 = jnp.bfloat16
 SMALL = pltpu.CompilerParams(vmem_limit_bytes=8 * 1024 * 1024)
@@ -25,6 +26,10 @@
     return lax.ppermute(array, axis, pairs)
 
 
+def parity(axis, turn):
+    return (lax.axis_index(axis) + turn) % 2
+
+
 def split(array):
     high = array.astype(BF16).astype(F32)
     return high, array - high
@@ -42,9 +47,9 @@
     return jnp.dot(left, right, preferred_element_type=F32)
 
 
-def tables_kernel(feat, coord, w_both, table_c, packed, send_far, send_near):
+def tables_kernel(feat, coord, w_center, w_neigh, table_c, packed, send_far, send_near):
     inner_x, inner_y, lat, slots = feat.shape
-    both = 0.5 * w_both[...].astype(F32)
+    both = jnp.concatenate([w_center[...].astype(F32), w_neigh[...].astype(F32)], 1)
     both = jnp.concatenate([both, both], 0).T.astype(BF16)
     pad = jnp.zeros((ROWS - lat - 3, slots), F32)
     for x in range(inner_x):
@@ -56,7 +61,7 @@
             table_c[x * inner_y + y] = piece[:lat]
             packed[x, y, :lat] = piece[lat:]
             packed[x, y, lat:] = jnp.concatenate([coord[x, m, y : y + 1] for m in range(3)] + [pad], 0)
-    odd = lax.axis_index("bx") % 2
+    odd = parity("bx", HALO_X)
     last = inner_x - 1
     send_far[...] = packed[last * odd]
     send_near[...] = packed[last * (1 - odd)]
@@ -74,25 +79,72 @@
             side,
         ),
         compiler_params=SMALL,
-    )(features, coords, jnp.concatenate([w_center, w_neigh], 1))
-
-
-def sides_kernel(packed, from_far, from_near, send_far, send_near):
+    )(0.5 * features, coords, w_center, w_neigh)
+
+
+def sides_kernel(
+    packed,
+    from_far,
+    from_near,
+    centers,
+    neighbours,
+    live,
+    w_radial,
+    w_latent,
+    w_tensor,
+    w_mix,
+    w_env,
+    w_out,
+    send_far,
+    send_near,
+    lists,
+    wr_all,
+    w_latent_o,
+    w_tensor_o,
+    w_mix_o,
+    w_env_o,
+    w_out_o,
+):
     inner_x, inner_y = packed.shape[:2]
-    odd_x = lax.axis_index("bx") % 2
-    odd_y = lax.axis_index("by") % 2
+    blocks, slots = centers.shape[2:]
+    odd_x = parity("bx", HALO_X)
+    odd_y = parity("by", HALO_Y)
     for send, odd in ((send_far, odd_y), (send_near, 1 - odd_y)):
         row = (inner_y - 1) * odd
         send[(inner_x + 1) * odd_x] = from_far[row]
         send[(inner_x + 1) * (1 - odd_x)] = from_near[row]
         for x in range(inner_x):
             send[x + 1] = packed[x, row]
-
-
-def sides(packed, from_far, from_near):
+    lists[:blocks] = centers[0, 0]
+    lists[blocks : 2 * blocks] = neighbours[0, 0]
+    lists[2 * blocks :] = jnp.broadcast_to(live[...], (8, slots))
+    high, low = split(0.5 * w_radial[...])
+    wr_all[...] = jnp.concatenate([high, high, low, low, high, low], 0).astype(BF16)
+    w_latent_o[...] = halved(w_latent[...])
+    w_tensor_o[...] = w_tensor[...]
+    w_mix_o[...] = w_mix[...]
+    w_env_o[...] = w_env[...]
+    w_out_o[...] = jnp.broadcast_to(w_out[...], (8, w_out.shape[1])).T[:, :1]
+
+
+def sides(packed, from_far, from_near, centers, neighbours, live, *weights):
     inner_x, _, rows, slots = packed.shape
+    blocks = centers.shape[2]
+    nb, lat = weights[0].shape
     send = jax.ShapeDtypeStruct((inner_x + 2, rows, slots), F32)
-    return pl.pallas_call(sides_kernel, out_shape=(send, send), compiler_params=SMALL)(packed, from_far, from_near)
+    same = [jax.ShapeDtypeStruct(w.shape, w.dtype) for w in weights]
+    return pl.pallas_call(
+        sides_kernel,
+        out_shape=(
+            send,
+            send,
+            jax.ShapeDtypeStruct((2 * blocks + 8, slots), jnp.int32),
+            jax.ShapeDtypeStruct((6 * nb, lat), BF16),
+            *same[1:5],
+            jax.ShapeDtypeStruct((lat, 1), F32),
+        ),
+        compiler_params=SMALL,
+    )(packed, from_far, from_near, centers, neighbours, live, *weights)
 
 
 def sine_cosine(turns):
@@ -121,18 +173,15 @@
 
 
 def brick_kernel(
-    cells,
-    live,
-    centers,
-    neighbours,
+    lists,
     table_c,
     packed,
     far_x,
     near_x,
     far_y,
     near_y,
-    w_radial,
-    w_latent,
+    wr_all,
+    half_latent,
     w_tensor,
     w_mix,
     w_env,
@@ -154,12 +203,13 @@
 ):
     inner_x, inner_y, _, slots = packed.shape
     wide_y = inner_y + 2
-    lat = w_latent.shape[0]
-    ch = w_tensor.shape[1]
-    nb = w_radial.shape[0]
+    lat = half_latent.shape[0]
+    ch = w_tensor.shape[0]
+    nb = wr_all.shape[0] // 6
+    count = (lists.shape[0] - 8) // 2
     width = GROUP * slots
-    odd_x = lax.axis_index("bx") % 2
-    odd_y = lax.axis_index("by") % 2
+    odd_x = parity("bx", HALO_X)
+    odd_y = parity("by", HALO_Y)
     far_x_at = (inner_x + 1) * odd_x
     near_x_at = (inner_x + 1) * (1 - odd_x)
     far_y_at = (inner_y + 1) * odd_y
@@ -176,10 +226,9 @@
     gamma[...] = jnp.zeros_like(gamma)
     g_gamma[...] = jnp.zeros_like(g_gamma)
     push[...] = jnp.zeros_like(push)
-    wr_high, wr_low = split(0.5 * w_radial[...])
-    half_latent, half_mix, half_env = halved(w_latent[...]), halved(w_mix[...]), halved(w_env[...])
-    wr_fwd = jnp.concatenate([wr_high, wr_high, wr_low, wr_low], 0).astype(BF16)
-    wr_bwd = jnp.concatenate([wr_high, wr_low], 0).astype(BF16)
+    wr_fwd, wr_bwd = wr_all[: 4 * nb], wr_all[4 * nb :]
+    half_mix, half_env = halved(w_mix[...]), halved(w_env[...])
+    live = lists[2 * count : 2 * count + 1, :1]
     orders = lax.broadcasted_iota(jnp.int32, (nb, 1), 0).astype(F32) + 1.0
     slot_iota = lax.broadcasted_iota(jnp.int32, (slots, slots), 0)
     row_iota = lax.broadcasted_iota(jnp.int32, (8, 1), 0)
@@ -187,11 +236,14 @@
     out_col = w_out[...]
     half_col = 0.5 * out_col
     offsets = [dx * wide_y + dy for dx in (-1, 0, 1) for dy in (-1, 0, 1)]
-    groups = (live[0, 0] + (GROUP - 1)) // GROUP
+    groups = count // GROUP
     block_iota = lax.broadcasted_iota(jnp.int32, (1, width), 1) // slots
 
+    heads = lists[:count, :1] >> 7
+    cells = [heads[block, 0] for block in range(count)]
+
     def cell_of(block):
-        cell = cells[0, block] // slots
+        cell = cells[block]
         cell_x = cell // inner_y
         return cell, (cell_x + 1) * wide_y + (cell - cell_x * inner_y) + 1
 
@@ -217,9 +269,9 @@
             table[cell] += sum(out[i : i + rows] for i in range(0, out.shape[0], rows))
 
     def forward(g, carry):
-        blocks = pl.multiple_of(g * GROUP, GROUP)
-        c_rows = centers[0, 0, pl.ds(blocks, GROUP), :] & (slots - 1)
-        n_all = neighbours[0, 0, pl.ds(blocks, GROUP), :]
+        blocks = 0
+        c_rows = lists[:GROUP] & (slots - 1)
+        n_all = lists[GROUP : 2 * GROUP]
         n_rows = n_all & (slots - 1)
         n_cells = n_all >> 7
         n_x = (n_cells * 43) >> 8
@@ -250,18 +302,18 @@
         inverse = lax.rsqrt(length2)
         scaled = jnp.minimum(length2 * inverse * (1.0 / CUTOFF), 1.0)
         fall = 1.0 - scaled * scaled
-        weight = jnp.where(block_iota + blocks < live[0, 0], fall * fall, 0.0)
+        weight = jnp.where(block_iota + blocks < live, fall * fall, 0.0)
         harm = delta * inverse
         basis, _ = sine_cosine(orders * scaled)
         b_high, b_low = split(basis)
         b_all = jnp.concatenate([b_high, b_low, b_high, b_low], 0).astype(BF16)
         zeta, slope = gated(near + dot_tn(wr_fwd, b_all))
         slope_z[g] = slope
-        latent, slope = gated(dot_tn(half_latent, zeta.astype(BF16)))
+        latent, slope = gated(dot_tn(half_latent[...], zeta.astype(BF16)))
         slope_l[g] = slope
         latent = latent.astype(BF16)
         latent_s[g] = latent
-        chan = dot_tn(w_tensor[...], latent)
+        chan = dot_nn(w_tensor[...], latent)
         chan_s[g] = chan
         rows_s[g, 0:3] = harm[0:3]
         rows_s[g, 3:4] = weight
@@ -275,8 +327,8 @@
     lax.fori_loop(0, groups, forward, 0)
 
     def middle(g, carry):
-        blocks = pl.multiple_of(g * GROUP, GROUP)
-        c_rows = centers[0, 0, pl.ds(blocks, GROUP), :] & (slots - 1)
+        blocks = 0
+        c_rows = lists[:GROUP] & (slots - 1)
         seen = gathered(gamma, c_rows, blocks)
         weight = rows_s[g, 3:4]
         harm = [rows_s[g, m : m + 1] for m in range(3)]
@@ -299,9 +351,9 @@
     lax.fori_loop(0, groups, middle, 0)
 
     def backward(g, carry):
-        blocks = pl.multiple_of(g * GROUP, GROUP)
-        c_rows = centers[0, 0, pl.ds(blocks, GROUP), :] & (slots - 1)
-        n_all = neighbours[0, 0, pl.ds(blocks, GROUP), :]
+        blocks = 0
+        c_rows = lists[:GROUP] & (slots - 1)
+        n_all = lists[GROUP : 2 * GROUP]
         n_rows = n_all & (slots - 1)
         n_cells = n_all >> 7
         back = gathered(g_gamma, c_rows, blocks)
@@ -325,14 +377,14 @@
                 g_chan = g_chan + part * harm[m - 1]
                 g_harm.append(rows_s[g, 7 + m : 8 + m] + weight * along)
         g_chan = (g_chan * weight).astype(BF16)
-        g_latent = dot_nn(w_mix[...], g_hidden_s[g]) + dot_nn(w_tensor[...], g_chan)
-        g_zeta = dot_nn(half_latent, (g_latent * slope_l[g]).astype(BF16))
+        g_latent = dot_nn(w_mix[...], g_hidden_s[g]) + dot_tn(w_tensor[...], g_chan)
+        g_zeta = dot_nn(half_latent[...], (g_latent * slope_l[g]).astype(BF16))
         g_pair = dot_nn(wr_bwd, (g_zeta * slope_z[g]).astype(BF16))
         _, cosines = sine_cosine(orders * scaled)
         turning = (3.14159265358979 * orders) * cosines
         g_scaled = jnp.sum((g_pair[:nb] + g_pair[nb:]) * turning, 0, keepdims=True)
         g_scaled = jnp.where(scaled < 1.0, g_scaled, 0.0)
-        g_weight = jnp.where(block_iota + blocks < live[0, 0], g_weight, 0.0)
+        g_weight = jnp.where(block_iota + blocks < live, g_weight, 0.0)
         g_scaled = g_scaled - 4.0 * scaled * (1.0 - scaled * scaled) * g_weight
         radial = g_harm[0] * harm[0] + g_harm[1] * harm[1] + g_harm[2] * harm[2]
         pull = g_scaled * (1.0 / CUTOFF) - radial * inverse
@@ -358,8 +410,10 @@
         both = push[cell]
         return both[0:4] + both[4:8]
 
+    odd_x = parity("bx", BACK_X)
+    far_at, near_at = (inner_x + 1) * odd_x, (inner_x + 1) * (1 - odd_x)
     for y in range(wide_y):
-        for target, x in ((push_far, far_x_at), (push_near, near_x_at)):
+        for target, x in ((push_far, far_at), (push_near, near_at)):
             sums = total(x * wide_y + y)
             for m in range(3):
                 target[m, y : y + 1] = sums[m : m + 1]
@@ -371,10 +425,10 @@
                 energies[x, y - 1 : y] = sums[3:4]
 
 
-def turned_kernel(inner, from_far, from_near, send_far, send_near, kept, work):
+def turned_kernel(inner, from_far, from_near, send_near, send_far, kept, work):
     inner_x, _, wide_y, _ = inner.shape
-    odd_x = lax.axis_index("bx") % 2
-    odd_y = lax.axis_index("by") % 2
+    odd_x = parity("bx", BACK_X)
+    odd_y = parity("by", BACK_Y)
     work[...] = inner[...]
     work[(inner_x - 1) * odd_x] += from_far[...]
     work[(inner_x - 1) * (1 - odd_x)] += from_near[...]
@@ -398,9 +452,9 @@
     )(inner, from_far, from_near)
 
 
-def final_kernel(kept, from_far, from_near, forces):
+def final_kernel(kept, from_near, from_far, forces):
     inner_x, _, inner_y, slots = kept.shape
-    odd_y = lax.axis_index("by") % 2
+    odd_y = parity("by", BACK_Y)
     rows = lax.broadcasted_iota(jnp.int32, (inner_y, slots), 0)
     far_at = (inner_y - 1) * odd_y
     near_at = (inner_y - 1) * (1 - odd_y)
@@ -411,27 +465,23 @@
             forces[x, m] = kept[x, m] + far + near
 
 
-def final(kept, from_far, from_near):
+def final(kept, from_near, from_far):
     return pl.pallas_call(
         final_kernel, out_shape=jax.ShapeDtypeStruct(kept.shape, F32), compiler_params=SMALL
-    )(kept, from_far, from_near)
-
-
-def brick(centers, neighbours, live_blocks, table_c, packed, far_x, near_x, far_y, near_y, *weights):
+    )(kept, from_near, from_far)
+
+
+def brick(lists, table_c, packed, far_x, near_x, far_y, near_y, *weights):
     inner_x, inner_y, rows, slots = packed.shape
-    blocks = centers.shape[2]
+    blocks = (lists.shape[0] - 8) // 2
     lat = table_c.shape[1]
-    ch = weights[2].shape[1]
+    ch = weights[2].shape[0]
     wide_y = inner_y + 2
     cells_ext = (inner_x + 2) * wide_y
     groups = blocks // GROUP
     width = GROUP * slots
-    vmem = pl.BlockSpec(memory_space=pltpu.VMEM)
-    smem = pl.BlockSpec(memory_space=pltpu.SMEM)
     return pl.pallas_call(
         brick_kernel,
-        in_specs=[smem, smem] + [vmem] * 14,
-        out_specs=(vmem,) * 4,
         out_shape=(
             jax.ShapeDtypeStruct((inner_x, inner_y, slots), F32),
             jax.ShapeDtypeStruct((3, wide_y, slots), F32),
@@ -451,7 +501,7 @@
             pltpu.VMEM((groups, 16, width), F32),
         ],
         compiler_params=pltpu.CompilerParams(vmem_limit_bytes=40 * 1024 * 1024),
-    )(centers[0, :, :, 0], live_blocks, centers, neighbours, table_c, packed, far_x, near_x, far_y, near_y, *weights)
+    )(lists, table_c, packed, far_x, near_x, far_y, near_y, *weights)
 
 
 def body(
@@ -471,21 +521,20 @@
 ):
     table_c, packed, send_far, send_near = tables(features, jnp.swapaxes(coords, 1, 2), w_center, w_neigh)
     inner_x, inner_y = packed.shape[:2]
-    far_x = swapped(send_far, "bx", 1)
-    near_x = swapped(send_near, "bx", 0)
-    send_far, send_near = sides(packed, far_x, near_x)
-    far_y = swapped(send_far, "by", 1)
-    near_y = swapped(send_near, "by", 0)
-    weights = (w_radial, w_latent, w_tensor, w_mix, w_env, w_out[:, None])
-    energies, push_far, push_near, inner = brick(
-        centers, neighbours, live_blocks, table_c, packed, far_x, near_x, far_y, near_y, *weights
-    )
-    from_far = swapped(push_far, "bx", 1)
-    from_near = swapped(push_near, "bx", 0)
-    send_far, send_near, kept = turned(inner, from_far, from_near)
-    from_far = swapped(send_far, "by", 1)
-    from_near = swapped(send_near, "by", 0)
-    forces = jnp.swapaxes(final(kept, from_far, from_near), 1, 2)
+    far_x = swapped(send_far, "bx", 1 - HALO_X)
+    near_x = swapped(send_near, "bx", HALO_X)
+    weights = (w_radial, w_latent, w_tensor.T, w_mix, w_env, w_out[None])
+    send_far, send_near, *operands = sides(packed, far_x, near_x, centers, neighbours, live_blocks, *weights)
+    far_y = swapped(send_far, "by", 1 - HALO_Y)
+    near_y = swapped(send_near, "by", HALO_Y)
+    lists, *weights = operands
+    energies, push_far, push_near, inner = brick(lists, table_c, packed, far_x, near_x, far_y, near_y, *weights)
+    from_far = swapped(push_far, "bx", 1 - BACK_X)
+    from_near = swapped(push_near, "bx", BACK_X)
+    send_near, send_far, kept = turned(inner, from_far, from_near)
+    from_near = swapped(send_near, "by", BACK_Y)
+    from_far = swapped(send_far, "by", 1 - BACK_Y)
+    forces = jnp.swapaxes(final(kept, from_near, from_far), 1, 2)
     return (energies, forces)
 
 

time: 64.1 us -> 63.5 us (level)
  waiting for transfers between devices: 7.69 us -> 10.3 us
  starting transfers between devices: 39.8 us -> 37.5 us
  local copies, waits for them, and re-layouts: 1.9 us -> 0.66 us
    ppermute x8, waiting for transfers between devices: 7.69 us -> 10.3 us  [swapped(): return lax.ppermute(array, axis, pairs)]
    ppermute x8, starting transfers between devices: 39.8 us -> 37.5 us  [swapped(): return lax.ppermute(array, axis, pairs)]
    mul x0 -> x1, other arithmetic: none -> 1.1 us  [tables(): 0.5 * features]
    unnamed x21 -> x22, local copies, waits for them, and re-layouts: 1.69 us -> 0.66 us
    concatenate x1 -> x0, other arithmetic: 0.82 us -> none  [tables(): jnp.concatenate([w_center, w_neigh], 1)]
  transfers between devices with their start and end apart: 8 -> 8, of which waited for: 5 -> 6; matrix products, arithmetic and copies ran while one was open for 0% -> 0% of each run, Pallas kernels for 0% -> 0%
where the time goes in v4:
time: 63.5 us; the launch traced here: 63.1 us
  starting transfers between devices  37.5 us (59%)
  Pallas kernels  12 us (19%)
  waiting for transfers between devices  10.3 us (16%)
  between operations  1.52 us (2%)
  other arithmetic  1.1 us (2%)
  local copies, waits for them, and re-layouts  0.66 us (1%)
    ppermute x8, starting transfers between devices, swapped(): return lax.ppermute(array, axis, pairs)  37.5 us
    pallas_call x1, Pallas kernels, brick(): pl.pallas_call(brick_kernel, out_shape=(jax.ShapeDtypeStruct((inner_x, in...  10.8 us
    ppermute x8, waiting for transfers between devices, swapped(): return lax.ppermute(array, axis, pairs)  10.3 us
  transfers between devices with their start and end apart: 8, of which 6 were waited for; matrix products, arithmetic and copies ran while one was open for 0% of the time, Pallas kernels for 0%

profile of v4, /device:TPU:1, one launch (start us, length us, event | category | flops | bytes accessed | tf_op | source)
XLA Modules:
  0.0 63.1 jit_solution(965729192123198267)
XLA Ops:
  0.6 0.0 copy-start.6
  0.6 0.0 copy-start.5
  0.7 0.0 copy-start
  0.7 1.1 %broadcast_multiply_fusion.feat = f32[4,4,64,128]{3,2,1,0:T(8,128)S(1)} fusion(f32[4,4,64,128]{3,2,1,0:T(8,128)} %param.13), kind=kLoop, calls=%fused_computation | loop fusion | flops 131072 | bytes 1048576 | tf_op jit(solution)/shard_map/mul | solution.py:82
  1.8 0.0 copy-done.6
  1.8 0.0 copy-done.5
  1.8 0.0 copy-done
  1.8 0.0 copy-start.1
  1.8 0.0 copy-start.2
  1.8 0.0 copy-start.3
  1.8 0.0 copy-start.4
  1.8 0.0 copy-start.9
  1.9 0.4 shard_map.140
  2.3 15.1 %collective-permute-start = (f32[4,72,128]{2,1,0:T(8,128)S(1)}, f32[4,72,128]{2,1,0:T(8,128)S(1)}, u32[]{:S(2)}, u32[]{:S(2)}) collective-permute-start(f32[4,72,128]{2,1,0:T(8,128)S(1)} %get-tuple-element.23), channel_id=1, source_target_pairs={{64,128},{128,64},{192,256},{256,192},{320,384},{384,320},{448,512... | collective-permute-start | bytes 442376 | tf_op jit(solution)/shard_map/ppermute | solution.py:26
  17.4 0.0 copy-start.8
  17.5 0.0 copy-start.7
  17.5 1.9 %collective-permute-start.1 = (f32[4,72,128]{2,1,0:T(8,128)S(1)}, f32[4,72,128]{2,1,0:T(8,128)S(1)}, u32[]{:S(2)}, u32[]{:S(2)}) collective-permute-start(f32[4,72,128]{2,1,0:T(8,128)S(1)} %get-tuple-element.24), channel_id=1, source_target_pairs={{0,64},{64,0},{128,192},{192,128},{256,320},{320,256},{384,448},{4... | collective-permute-start | bytes 442376 | tf_op jit(solution)/shard_map/ppermute | solution.py:26
  20.0 1.0 %collective-permute-done.from_far.far_x = f32[4,72,128]{2,1,0:T(8,128)S(1)} collective-permute-done((f32[4,72,128]{2,1,0:T(8,128)S(1)}, f32[4,72,128]{2,1,0:T(8,128)S(1)}, u32[]{:S(2)}, u32[]{:S(2)}) %collective-permute-start) | collective-permute-done | bytes 147488 | tf_op jit(solution)/shard_map/ppermute | solution.py:26
  21.0 2.8 %collective-permute-done.1.from_near.near_x = f32[4,72,128]{2,1,0:T(8,128)S(1)} collective-permute-done((f32[4,72,128]{2,1,0:T(8,128)S(1)}, f32[4,72,128]{2,1,0:T(8,128)S(1)}, u32[]{:S(2)}, u32[]{:S(2)}) %collective-permute-start.1) | collective-permute-done | bytes 147488 | tf_op jit(solution)/shard_map/ppermute | solution.py:26
  23.8 0.0 copy-start.10
  23.8 0.0 copy-done.1
  23.8 0.0 copy-done.2
  23.8 0.0 copy-done.3
  23.8 0.0 copy-done.4
  23.8 0.0 copy-done.9
  23.8 0.0 copy-done.8
  23.8 0.0 copy-done.7
  23.8 0.6 copy-done.10
  24.4 0.1 shard_map.141
  24.5 4.9 %collective-permute-start.2 = (f32[6,72,128]{2,1,0:T(8,128)S(1)}, f32[6,72,128]{2,1,0:T(8,128)S(1)}, u32[]{:S(2)}, u32[]{:S(2)}) collective-permute-start(f32[6,72,128]{2,1,0:T(8,128)S(1)} %get-tuple-element.27), channel_id=1, source_target_pairs={{1,2},{2,1},{3,4},{4,3},{5,6},{6,5},{7,8},{8,7},{9,10},{10,9},{11,... | collective-permute-start | bytes 663560 | tf_op jit(solution)/shard_map/ppermute | solution.py:26
  29.5 4.6 %collective-permute-start.3 = (f32[6,72,128]{2,1,0:T(8,128)S(1)}, f32[6,72,128]{2,1,0:T(8,128)S(1)}, u32[]{:S(2)}, u32[]{:S(2)}) collective-permute-start(f32[6,72,128]{2,1,0:T(8,128)S(1)} %get-tuple-element.28), channel_id=1, source_target_pairs={{0,1},{1,0},{2,3},{3,2},{4,5},{5,4},{6,7},{7,6},{8,9},{9,8},{10,11... | collective-permute-start | bytes 663560 | tf_op jit(solution)/shard_map/ppermute | solution.py:26
  34.1 0.0 collective-permute-done.2.far_y
  34.1 1.1 %collective-permute-done.3.near_y = f32[6,72,128]{2,1,0:T(8,128)S(1)} collective-permute-done((f32[6,72,128]{2,1,0:T(8,128)S(1)}, f32[6,72,128]{2,1,0:T(8,128)S(1)}, u32[]{:S(2)}, u32[]{:S(2)}) %collective-permute-start.3) | collective-permute-done | bytes 221216 | tf_op jit(solution)/shard_map/ppermute | solution.py:26
  35.2 10.8 %shard_map.142 = (f32[4,4,128]{2,1,0:T(4,128)}, f32[3,6,128]{2,1,0:T(8,128)S(1)}, f32[3,6,128]{2,1,0:T(8,128)S(1)}, f32[4,3,6,128]{3,2,1,0:T(8,128)S(1)}) custom-call(s32[72,128]{1,0:T(8,128)S(1)} %get-tuple-element.25.lists, f32[16,64,128]{2,1,0:T(8,128)S(1)} %get-tuple-element.26.table_c, f32[4,4,72,128]{3,2,1,0:T(8,128)S(1)} %get-tuple-element.22.packed, ...), custom_call_target="tpu_custom_call" | custom-call | tf_op jit(solution)/shard_map/pallas_call | solution.py:483
  46.1 2.2 %collective-permute-start.4 = (f32[3,6,128]{2,1,0:T(8,128)S(1)}, f32[3,6,128]{2,1,0:T(8,128)S(1)}, u32[]{:S(2)}, u32[]{:S(2)}) collective-permute-start(f32[3,6,128]{2,1,0:T(8,128)S(1)} %get-tuple-element.37), channel_id=1, source_target_pairs={{64,128},{128,64},{192,256},{256,192},{320,384},{384,320},{448,512... | collective-permute-start | bytes 27656 | tf_op jit(solution)/shard_map/ppermute | solution.py:26
  48.3 1.9 %collective-permute-start.5 = (f32[3,6,128]{2,1,0:T(8,128)S(1)}, f32[3,6,128]{2,1,0:T(8,128)S(1)}, u32[]{:S(2)}, u32[]{:S(2)}) collective-permute-start(f32[3,6,128]{2,1,0:T(8,128)S(1)} %get-tuple-element.38), channel_id=1, source_target_pairs={{0,64},{64,0},{128,192},{192,128},{256,320},{320,256},{384,448},{4... | collective-permute-start | bytes 27656 | tf_op jit(solution)/shard_map/ppermute | solution.py:26
  50.2 1.5 %collective-permute-done.4.from_far = f32[3,6,128]{2,1,0:T(8,128)S(1)} collective-permute-done((f32[3,6,128]{2,1,0:T(8,128)S(1)}, f32[3,6,128]{2,1,0:T(8,128)S(1)}, u32[]{:S(2)}, u32[]{:S(2)}) %collective-permute-start.4) | collective-permute-done | bytes 9248 | tf_op jit(solution)/shard_map/ppermute | solution.py:26
  51.7 1.0 %collective-permute-done.5.from_near = f32[3,6,128]{2,1,0:T(8,128)S(1)} collective-permute-done((f32[3,6,128]{2,1,0:T(8,128)S(1)}, f32[3,6,128]{2,1,0:T(8,128)S(1)}, u32[]{:S(2)}, u32[]{:S(2)}) %collective-permute-start.5) | collective-permute-done | bytes 9248 | tf_op jit(solution)/shard_map/ppermute | solution.py:26
  52.8 4.8 %collective-permute-start.6 = (f32[4,3,128]{2,1,0:T(4,128)S(1)}, f32[4,3,128]{2,1,0:T(4,128)S(1)}, u32[]{:S(2)}, u32[]{:S(2)}) collective-permute-start(f32[4,3,128]{2,1,0:T(4,128)S(1)} %get-tuple-element.40), channel_id=1, source_target_pairs={{0,1},{1,0},{2,3},{3,2},{4,5},{5,4},{6,7},{7,6},{8,9},{9,8},{10,11... | collective-permute-start | bytes 18440 | tf_op jit(solution)/shard_map/ppermute | solution.py:26
  57.5 1.9 %collective-permute-start.7 = (f32[4,3,128]{2,1,0:T(4,128)S(1)}, f32[4,3,128]{2,1,0:T(4,128)S(1)}, u32[]{:S(2)}, u32[]{:S(2)}) collective-permute-start(f32[4,3,128]{2,1,0:T(4,128)S(1)} %get-tuple-element.41), channel_id=1, source_target_pairs={{1,2},{2,1},{3,4},{4,3},{5,6},{6,5},{7,8},{8,7},{9,10},{10,9},{11,... | collective-permute-start | bytes 18440 | tf_op jit(solution)/shard_map/ppermute | solution.py:26
  59.5 0.0 collective-permute-done.6.from_near
  59.5 3.0 %collective-permute-done.7.from_far = f32[4,3,128]{2,1,0:T(4,128)S(1)} collective-permute-done((f32[4,3,128]{2,1,0:T(4,128)S(1)}, f32[4,3,128]{2,1,0:T(4,128)S(1)}, u32[]{:S(2)}, u32[]{:S(2)}) %collective-permute-start.7) | collective-permute-done | bytes 6176 | tf_op jit(solution)/shard_map/ppermute | solution.py:26
  62.5 0.6 shard_map.144
  (1 shorter events, 0.0 us)
Async XLA Ops:
  0.6 1.1 %copy-start.6 = (bf16[64,64]{1,0:T(8,128)(2,1)S(1)}, bf16[64,64]{1,0:T(8,128)(2,1)}, u32[]{:S(2)}) copy-start(bf16[64,64]{1,0:T(8,128)(2,1)} %w_neigh.1) | copy-start | bytes 24580
  0.6 1.1 %copy-start.5 = (bf16[64,64]{1,0:T(8,128)(2,1)S(1)}, bf16[64,64]{1,0:T(8,128)(2,1)}, u32[]{:S(2)}) copy-start(bf16[64,64]{1,0:T(8,128)(2,1)} %w_center.1) | copy-start | bytes 24580
  0.7 1.1 %copy-start = (f32[4,4,3,128]{3,1,2,0:T(4,128)S(1)}, f32[4,4,3,128]{3,1,2,0:T(4,128)}, u32[]{:S(2)}) copy-start(f32[4,4,3,128]{3,1,2,0:T(4,128)} %param.14) | copy-start | bytes 73732
  1.8 22.0 %copy-start.1 = (s32[1,1,32,128]{3,2,1,0:T(8,128)S(1)}, s32[1,1,32,128]{3,2,1,0:T(8,128)}, u32[]{:S(2)}) copy-start(s32[1,1,32,128]{3,2,1,0:T(8,128)} %centers.1) | copy-start | bytes 49156
  1.8 22.0 %copy-start.2 = (s32[1,1,32,128]{3,2,1,0:T(8,128)S(1)}, s32[1,1,32,128]{3,2,1,0:T(8,128)}, u32[]{:S(2)}) copy-start(s32[1,1,32,128]{3,2,1,0:T(8,128)} %neighbours.1) | copy-start | bytes 49156
  1.8 22.0 %copy-start.3 = (bf16[64,64]{1,0:T(8,128)(2,1)S(1)}, bf16[64,64]{1,0:T(8,128)(2,1)}, u32[]{:S(2)}) copy-start(bf16[64,64]{1,0:T(8,128)(2,1)} %w_latent.1) | copy-start | bytes 24580
  1.8 21.9 %copy-start.4 = (bf16[64,64]{1,0:T(8,128)(2,1)S(1)}, bf16[64,64]{1,0:T(8,128)(2,1)}, u32[]{:S(2)}) copy-start(bf16[64,64]{1,0:T(8,128)(2,1)} %w_mix.1) | copy-start | bytes 24580
  1.8 21.9 %copy-start.9 = (bf16[16,64]{1,0:T(8,128)(2,1)S(1)}, bf16[16,64]{1,0:T(8,128)(2,1)}, u32[]{:S(2)}) copy-start(bf16[16,64]{1,0:T(8,128)(2,1)} %w_env.1) | copy-start | bytes 6148
  2.3 18.7 %collective-permute-start = (f32[4,72,128]{2,1,0:T(8,128)S(1)}, f32[4,72,128]{2,1,0:T(8,128)S(1)}, u32[]{:S(2)}, u32[]{:S(2)}) collective-permute-start(f32[4,72,128]{2,1,0:T(8,128)S(1)} %get-tuple-element.23), channel_id=1, source_target_pairs={{64,128},{128,64},{192,256},{256,192},{320,384},{384,320},{448,512... | collective-permute-start | bytes 442376 | tf_op jit(solution)/shard_map/ppermute | solution.py:26
  17.4 6.4 %copy-start.8 = (bf16[64,16]{0,1:T(8,128)(2,1)S(1)}, bf16[64,16]{0,1:T(8,128)(2,1)}, u32[]{:S(2)}) copy-start(bf16[64,16]{0,1:T(8,128)(2,1)} %param.22) | copy-start | bytes 6148
  17.5 6.3 %copy-start.7 = (f32[8,64]{1,0:T(8,128)S(1)}, f32[8,64]{1,0:T(8,128)}, u32[]{:S(2)}) copy-start(f32[8,64]{1,0:T(8,128)} %w_radial.1) | copy-start | bytes 6148
  17.5 6.3 %collective-permute-start.1 = (f32[4,72,128]{2,1,0:T(8,128)S(1)}, f32[4,72,128]{2,1,0:T(8,128)S(1)}, u32[]{:S(2)}, u32[]{:S(2)}) collective-permute-start(f32[4,72,128]{2,1,0:T(8,128)S(1)} %get-tuple-element.24), channel_id=1, source_target_pairs={{0,64},{64,0},{128,192},{192,128},{256,320},{320,256},{384,448},{4... | collective-permute-start | bytes 442376 | tf_op jit(solution)/shard_map/ppermute | solution.py:26
  23.8 0.7 %copy-start.10 = (f32[64]{0:T(128)S(1)}, f32[64]{0:T(128)}, u32[]{:S(2)}) copy-start(f32[64]{0:T(128)} %param.25) | copy-start | bytes 772
  24.5 9.6 %collective-permute-start.2 = (f32[6,72,128]{2,1,0:T(8,128)S(1)}, f32[6,72,128]{2,1,0:T(8,128)S(1)}, u32[]{:S(2)}, u32[]{:S(2)}) collective-permute-start(f32[6,72,128]{2,1,0:T(8,128)S(1)} %get-tuple-element.27), channel_id=1, source_target_pairs={{1,2},{2,1},{3,4},{4,3},{5,6},{6,5},{7,8},{8,7},{9,10},{10,9},{11,... | collective-permute-start | bytes 663560 | tf_op jit(solution)/shard_map/ppermute | solution.py:26
  29.5 5.7 %collective-permute-start.3 = (f32[6,72,128]{2,1,0:T(8,128)S(1)}, f32[6,72,128]{2,1,0:T(8,128)S(1)}, u32[]{:S(2)}, u32[]{:S(2)}) collective-permute-start(f32[6,72,128]{2,1,0:T(8,128)S(1)} %get-tuple-element.28), channel_id=1, source_target_pairs={{0,1},{1,0},{2,3},{3,2},{4,5},{5,4},{6,7},{7,6},{8,9},{9,8},{10,11... | collective-permute-start | bytes 663560 | tf_op jit(solution)/shard_map/ppermute | solution.py:26
  46.1 5.6 %collective-permute-start.4 = (f32[3,6,128]{2,1,0:T(8,128)S(1)}, f32[3,6,128]{2,1,0:T(8,128)S(1)}, u32[]{:S(2)}, u32[]{:S(2)}) collective-permute-start(f32[3,6,128]{2,1,0:T(8,128)S(1)} %get-tuple-element.37), channel_id=1, source_target_pairs={{64,128},{128,64},{192,256},{256,192},{320,384},{384,320},{448,512... | collective-permute-start | bytes 27656 | tf_op jit(solution)/shard_map/ppermute | solution.py:26
  48.3 4.4 %collective-permute-start.5 = (f32[3,6,128]{2,1,0:T(8,128)S(1)}, f32[3,6,128]{2,1,0:T(8,128)S(1)}, u32[]{:S(2)}, u32[]{:S(2)}) collective-permute-start(f32[3,6,128]{2,1,0:T(8,128)S(1)} %get-tuple-element.38), channel_id=1, source_target_pairs={{0,64},{64,0},{128,192},{192,128},{256,320},{320,256},{384,448},{4... | collective-permute-start | bytes 27656 | tf_op jit(solution)/shard_map/ppermute | solution.py:26
  52.8 6.7 %collective-permute-start.6 = (f32[4,3,128]{2,1,0:T(4,128)S(1)}, f32[4,3,128]{2,1,0:T(4,128)S(1)}, u32[]{:S(2)}, u32[]{:S(2)}) collective-permute-start(f32[4,3,128]{2,1,0:T(4,128)S(1)} %get-tuple-element.40), channel_id=1, source_target_pairs={{0,1},{1,0},{2,3},{3,2},{4,5},{5,4},{6,7},{7,6},{8,9},{9,8},{10,11... | collective-permute-start | bytes 18440 | tf_op jit(solution)/shard_map/ppermute | solution.py:26
  57.5 5.0 %collective-permute-start.7 = (f32[4,3,128]{2,1,0:T(4,128)S(1)}, f32[4,3,128]{2,1,0:T(4,128)S(1)}, u32[]{:S(2)}, u32[]{:S(2)}) collective-permute-start(f32[4,3,128]{2,1,0:T(4,128)S(1)} %get-tuple-element.41), channel_id=1, source_target_pairs={{1,2},{2,1},{3,4},{4,3},{5,6},{6,5},{7,8},{8,7},{9,10},{10,9},{11,... | collective-permute-start | bytes 18440 | tf_op jit(solution)/shard_map/ppermute | solution.py:26

commit v5 on v4

--- a/solution.py
+++ b/solution.py
@@ -94,7 +94,6 @@
     w_tensor,
     w_mix,
     w_env,
-    w_out,
     send_far,
     send_near,
     lists,
@@ -118,19 +117,20 @@
     lists[:blocks] = centers[0, 0]
     lists[blocks : 2 * blocks] = neighbours[0, 0]
     lists[2 * blocks :] = jnp.broadcast_to(live[...], (8, slots))
-    high, low = split(0.5 * w_radial[...])
+    nb = w_radial.shape[0] - 1
+    high, low = split(0.5 * w_radial[:nb])
     wr_all[...] = jnp.concatenate([high, high, low, low, high, low], 0).astype(BF16)
     w_latent_o[...] = halved(w_latent[...])
     w_tensor_o[...] = w_tensor[...]
     w_mix_o[...] = w_mix[...]
     w_env_o[...] = w_env[...]
-    w_out_o[...] = jnp.broadcast_to(w_out[...], (8, w_out.shape[1])).T[:, :1]
+    w_out_o[...] = jnp.broadcast_to(w_radial[nb:], (8, w_radial.shape[1])).T[:, :1]
 
 
 def sides(packed, from_far, from_near, centers, neighbours, live, *weights):
     inner_x, _, rows, slots = packed.shape
     blocks = centers.shape[2]
-    nb, lat = weights[0].shape
+    nb, lat = weights[0].shape[0] - 1, weights[0].shape[1]
     send = jax.ShapeDtypeStruct((inner_x + 2, rows, slots), F32)
     same = [jax.ShapeDtypeStruct(w.shape, w.dtype) for w in weights]
     return pl.pallas_call(
@@ -140,7 +140,7 @@
             send,
             jax.ShapeDtypeStruct((2 * blocks + 8, slots), jnp.int32),
             jax.ShapeDtypeStruct((6 * nb, lat), BF16),
-            *same[1:5],
+            *same[1:],
             jax.ShapeDtypeStruct((lat, 1), F32),
         ),
         compiler_params=SMALL,
@@ -523,7 +523,7 @@
     inner_x, inner_y = packed.shape[:2]
     far_x = swapped(send_far, "bx", 1 - HALO_X)
     near_x = swapped(send_near, "bx", HALO_X)
-    weights = (w_radial, w_latent, w_tensor.T, w_mix, w_env, w_out[None])
+    weights = (jnp.concatenate([w_radial, w_out[None]], 0), w_latent, w_tensor.T, w_mix, w_env)
     send_far, send_near, *operands = sides(packed, far_x, near_x, centers, neighbours, live_blocks, *weights)
     far_y = swapped(send_far, "by", 1 - HALO_Y)
     near_y = swapped(send_near, "by", HALO_Y)

time: 63.5 us -> 62.9 us (level)
  no operation moved by 1% of the time
where the time goes in v5:
time: 62.9 us; the launch traced here: 62.5 us
  starting transfers between devices  37.5 us (60%)
  Pallas kernels  12.1 us (19%)
  waiting for transfers between devices  10.3 us (16%)
  between operations  1.54 us (2%)
  other arithmetic  1.1 us (2%)
    ppermute x8, starting transfers between devices, swapped(): return lax.ppermute(array, axis, pairs)  37.5 us
    pallas_call x1, Pallas kernels, brick(): pl.pallas_call(brick_kernel, out_shape=(jax.ShapeDtypeStruct((inner_x, in...  10.9 us
    ppermute x8, waiting for transfers between devices, swapped(): return lax.ppermute(array, axis, pairs)  10.3 us
  transfers between devices with their start and end apart: 8, of which 6 were waited for; matrix products, arithmetic and copies ran while one was open for 0% of the time, Pallas kernels for 0%

profile of v5, /device:TPU:1, one launch (start us, length us, event | category | flops | bytes accessed | tf_op | source)
XLA Modules:
  0.0 62.5 jit_solution(14654395270593069539)
XLA Ops:
  0.6 0.0 copy-start.6
  0.6 0.0 copy-start.5
  0.7 0.0 copy-start
  0.7 1.1 %broadcast_multiply_fusion.feat = f32[4,4,64,128]{3,2,1,0:T(8,128)S(1)} fusion(f32[4,4,64,128]{3,2,1,0:T(8,128)} %param.13), kind=kLoop, calls=%fused_computation | loop fusion | flops 131072 | bytes 1048576 | tf_op jit(solution)/shard_map/mul | solution.py:82
  1.8 0.0 copy-done.6
  1.8 0.0 copy-done.5
  1.8 0.0 copy-done
  1.8 0.0 copy-start.9
  1.8 0.0 copy-start.10
  1.8 0.0 copy-start.2
  1.8 0.0 copy-start.3
  1.8 0.0 copy-start.4
  1.9 0.0 copy-start.8
  1.9 0.4 shard_map.140
  2.3 0.0 copy-start.1
  2.3 15.1 %collective-permute-start = (f32[4,72,128]{2,1,0:T(8,128)S(1)}, f32[4,72,128]{2,1,0:T(8,128)S(1)}, u32[]{:S(2)}, u32[]{:S(2)}) collective-permute-start(f32[4,72,128]{2,1,0:T(8,128)S(1)} %get-tuple-element.23), channel_id=1, source_target_pairs={{64,128},{128,64},{192,256},{256,192},{320,384},{384,320},{448,512... | collective-permute-start | bytes 442376 | tf_op jit(solution)/shard_map/ppermute | solution.py:26
  17.5 1.9 %collective-permute-start.1 = (f32[4,72,128]{2,1,0:T(8,128)S(1)}, f32[4,72,128]{2,1,0:T(8,128)S(1)}, u32[]{:S(2)}, u32[]{:S(2)}) collective-permute-start(f32[4,72,128]{2,1,0:T(8,128)S(1)} %get-tuple-element.24), channel_id=1, source_target_pairs={{0,64},{64,0},{128,192},{192,128},{256,320},{320,256},{384,448},{4... | collective-permute-start | bytes 442376 | tf_op jit(solution)/shard_map/ppermute | solution.py:26
  20.0 0.0 copy-done.9
  20.1 0.0 copy-done.10
  20.1 0.0 copy-start.7
  20.1 0.9 %collective-permute-done.from_far.far_x = f32[4,72,128]{2,1,0:T(8,128)S(1)} collective-permute-done((f32[4,72,128]{2,1,0:T(8,128)S(1)}, f32[4,72,128]{2,1,0:T(8,128)S(1)}, u32[]{:S(2)}, u32[]{:S(2)}) %collective-permute-start) | collective-permute-done | bytes 147488 | tf_op jit(solution)/shard_map/ppermute | solution.py:26
  21.0 2.7 %collective-permute-done.1.from_near.near_x = f32[4,72,128]{2,1,0:T(8,128)S(1)} collective-permute-done((f32[4,72,128]{2,1,0:T(8,128)S(1)}, f32[4,72,128]{2,1,0:T(8,128)S(1)}, u32[]{:S(2)}, u32[]{:S(2)}) %collective-permute-start.1) | collective-permute-done | bytes 147488 | tf_op jit(solution)/shard_map/ppermute | solution.py:26
  23.8 0.0 copy-done.2
  23.8 0.0 copy-done.3
  23.8 0.0 copy-done.4
  23.8 0.0 copy-done.8
  23.8 0.0 copy-done.1
  23.8 0.0 copy-done.7
  23.8 0.1 shard_map.141
  23.9 4.9 %collective-permute-start.2 = (f32[6,72,128]{2,1,0:T(8,128)S(1)}, f32[6,72,128]{2,1,0:T(8,128)S(1)}, u32[]{:S(2)}, u32[]{:S(2)}) collective-permute-start(f32[6,72,128]{2,1,0:T(8,128)S(1)} %get-tuple-element.27), channel_id=1, source_target_pairs={{1,2},{2,1},{3,4},{4,3},{5,6},{6,5},{7,8},{8,7},{9,10},{10,9},{11,... | collective-permute-start | bytes 663560 | tf_op jit(solution)/shard_map/ppermute | solution.py:26
  28.9 4.6 %collective-permute-start.3 = (f32[6,72,128]{2,1,0:T(8,128)S(1)}, f32[6,72,128]{2,1,0:T(8,128)S(1)}, u32[]{:S(2)}, u32[]{:S(2)}) collective-permute-start(f32[6,72,128]{2,1,0:T(8,128)S(1)} %get-tuple-element.28), channel_id=1, source_target_pairs={{0,1},{1,0},{2,3},{3,2},{4,5},{5,4},{6,7},{7,6},{8,9},{9,8},{10,11... | collective-permute-start | bytes 663560 | tf_op jit(solution)/shard_map/ppermute | solution.py:26
  33.5 0.0 collective-permute-done.2.far_y
  33.5 1.1 %collective-permute-done.3.near_y = f32[6,72,128]{2,1,0:T(8,128)S(1)} collective-permute-done((f32[6,72,128]{2,1,0:T(8,128)S(1)}, f32[6,72,128]{2,1,0:T(8,128)S(1)}, u32[]{:S(2)}, u32[]{:S(2)}) %collective-permute-start.3) | collective-permute-done | bytes 221216 | tf_op jit(solution)/shard_map/ppermute | solution.py:26
  34.6 10.9 %shard_map.142 = (f32[4,4,128]{2,1,0:T(4,128)}, f32[3,6,128]{2,1,0:T(8,128)S(1)}, f32[3,6,128]{2,1,0:T(8,128)S(1)}, f32[4,3,6,128]{3,2,1,0:T(8,128)S(1)}) custom-call(s32[72,128]{1,0:T(8,128)S(1)} %get-tuple-element.25.lists, f32[16,64,128]{2,1,0:T(8,128)S(1)} %get-tuple-element.26.table_c, f32[4,4,72,128]{3,2,1,0:T(8,128)S(1)} %get-tuple-element.22.packed, ...), custom_call_target="tpu_custom_call" | custom-call | tf_op jit(solution)/shard_map/pallas_call | solution.py:483
  45.5 2.2 %collective-permute-start.4 = (f32[3,6,128]{2,1,0:T(8,128)S(1)}, f32[3,6,128]{2,1,0:T(8,128)S(1)}, u32[]{:S(2)}, u32[]{:S(2)}) collective-permute-start(f32[3,6,128]{2,1,0:T(8,128)S(1)} %get-tuple-element.37), channel_id=1, source_target_pairs={{64,128},{128,64},{192,256},{256,192},{320,384},{384,320},{448,512... | collective-permute-start | bytes 27656 | tf_op jit(solution)/shard_map/ppermute | solution.py:26
  47.7 1.9 %collective-permute-start.5 = (f32[3,6,128]{2,1,0:T(8,128)S(1)}, f32[3,6,128]{2,1,0:T(8,128)S(1)}, u32[]{:S(2)}, u32[]{:S(2)}) collective-permute-start(f32[3,6,128]{2,1,0:T(8,128)S(1)} %get-tuple-element.38), channel_id=1, source_target_pairs={{0,64},{64,0},{128,192},{192,128},{256,320},{320,256},{384,448},{4... | collective-permute-start | bytes 27656 | tf_op jit(solution)/shard_map/ppermute | solution.py:26
  49.6 1.5 %collective-permute-done.4.from_far = f32[3,6,128]{2,1,0:T(8,128)S(1)} collective-permute-done((f32[3,6,128]{2,1,0:T(8,128)S(1)}, f32[3,6,128]{2,1,0:T(8,128)S(1)}, u32[]{:S(2)}, u32[]{:S(2)}) %collective-permute-start.4) | collective-permute-done | bytes 9248 | tf_op jit(solution)/shard_map/ppermute | solution.py:26
  51.1 1.0 %collective-permute-done.5.from_near = f32[3,6,128]{2,1,0:T(8,128)S(1)} collective-permute-done((f32[3,6,128]{2,1,0:T(8,128)S(1)}, f32[3,6,128]{2,1,0:T(8,128)S(1)}, u32[]{:S(2)}, u32[]{:S(2)}) %collective-permute-start.5) | collective-permute-done | bytes 9248 | tf_op jit(solution)/shard_map/ppermute | solution.py:26
  52.2 4.8 %collective-permute-start.6 = (f32[4,3,128]{2,1,0:T(4,128)S(1)}, f32[4,3,128]{2,1,0:T(4,128)S(1)}, u32[]{:S(2)}, u32[]{:S(2)}) collective-permute-start(f32[4,3,128]{2,1,0:T(4,128)S(1)} %get-tuple-element.40), channel_id=1, source_target_pairs={{0,1},{1,0},{2,3},{3,2},{4,5},{5,4},{6,7},{7,6},{8,9},{9,8},{10,11... | collective-permute-start | bytes 18440 | tf_op jit(solution)/shard_map/ppermute | solution.py:26
  56.9 1.9 %collective-permute-start.7 = (f32[4,3,128]{2,1,0:T(4,128)S(1)}, f32[4,3,128]{2,1,0:T(4,128)S(1)}, u32[]{:S(2)}, u32[]{:S(2)}) collective-permute-start(f32[4,3,128]{2,1,0:T(4,128)S(1)} %get-tuple-element.41), channel_id=1, source_target_pairs={{1,2},{2,1},{3,4},{4,3},{5,6},{6,5},{7,8},{8,7},{9,10},{10,9},{11,... | collective-permute-start | bytes 18440 | tf_op jit(solution)/shard_map/ppermute | solution.py:26
  58.9 0.0 collective-permute-done.6.from_near
  58.9 3.0 %collective-permute-done.7.from_far = f32[4,3,128]{2,1,0:T(4,128)S(1)} collective-permute-done((f32[4,3,128]{2,1,0:T(4,128)S(1)}, f32[4,3,128]{2,1,0:T(4,128)S(1)}, u32[]{:S(2)}, u32[]{:S(2)}) %collective-permute-start.7) | collective-permute-done | bytes 6176 | tf_op jit(solution)/shard_map/ppermute | solution.py:26
  61.9 0.6 shard_map.144
  (2 shorter events, 0.0 us)
Async XLA Ops:
  0.6 1.1 %copy-start.6 = (bf16[64,64]{1,0:T(8,128)(2,1)S(1)}, bf16[64,64]{1,0:T(8,128)(2,1)}, u32[]{:S(2)}) copy-start(bf16[64,64]{1,0:T(8,128)(2,1)} %w_neigh.1) | copy-start | bytes 24580
  0.6 1.1 %copy-start.5 = (bf16[64,64]{1,0:T(8,128)(2,1)S(1)}, bf16[64,64]{1,0:T(8,128)(2,1)}, u32[]{:S(2)}) copy-start(bf16[64,64]{1,0:T(8,128)(2,1)} %w_center.1) | copy-start | bytes 24580
  0.7 1.1 %copy-start = (f32[4,4,3,128]{3,1,2,0:T(4,128)S(1)}, f32[4,4,3,128]{3,1,2,0:T(4,128)}, u32[]{:S(2)}) copy-start(f32[4,4,3,128]{3,1,2,0:T(4,128)} %param.14) | copy-start | bytes 73732
  1.8 18.2 %copy-start.9 = (f32[8,64]{1,0:T(8,128)S(1)}, f32[8,64]{1,0:T(8,128)}, u32[]{:S(2)}) copy-start(f32[8,64]{1,0:T(8,128)} %param.20) | copy-start | bytes 6148
  1.8 18.2 %copy-start.10 = (f32[64]{0:T(128)S(1)}, f32[64]{0:T(128)}, u32[]{:S(2)}) copy-start(f32[64]{0:T(128)} %param.25) | copy-start | bytes 772
  1.8 21.9 %copy-start.2 = (s32[1,1,32,128]{3,2,1,0:T(8,128)S(1)}, s32[1,1,32,128]{3,2,1,0:T(8,128)}, u32[]{:S(2)}) copy-start(s32[1,1,32,128]{3,2,1,0:T(8,128)} %neighbours.1) | copy-start | bytes 49156
  1.8 21.9 %copy-start.3 = (bf16[64,64]{1,0:T(8,128)(2,1)S(1)}, bf16[64,64]{1,0:T(8,128)(2,1)}, u32[]{:S(2)}) copy-start(bf16[64,64]{1,0:T(8,128)(2,1)} %w_latent.1) | copy-start | bytes 24580
  1.8 21.9 %copy-start.4 = (bf16[64,64]{1,0:T(8,128)(2,1)S(1)}, bf16[64,64]{1,0:T(8,128)(2,1)}, u32[]{:S(2)}) copy-start(bf16[64,64]{1,0:T(8,128)(2,1)} %w_mix.1) | copy-start | bytes 24580
  1.9 21.9 %copy-start.8 = (bf16[16,64]{1,0:T(8,128)(2,1)S(1)}, bf16[16,64]{1,0:T(8,128)(2,1)}, u32[]{:S(2)}) copy-start(bf16[16,64]{1,0:T(8,128)(2,1)} %w_env.1) | copy-start | bytes 6148
  2.3 21.5 %copy-start.1 = (s32[1,1,32,128]{3,2,1,0:T(8,128)S(1)}, s32[1,1,32,128]{3,2,1,0:T(8,128)}, u32[]{:S(2)}) copy-start(s32[1,1,32,128]{3,2,1,0:T(8,128)} %centers.1) | copy-start | bytes 49156
  2.3 18.7 %collective-permute-start = (f32[4,72,128]{2,1,0:T(8,128)S(1)}, f32[4,72,128]{2,1,0:T(8,128)S(1)}, u32[]{:S(2)}, u32[]{:S(2)}) collective-permute-start(f32[4,72,128]{2,1,0:T(8,128)S(1)} %get-tuple-element.23), channel_id=1, source_target_pairs={{64,128},{128,64},{192,256},{256,192},{320,384},{384,320},{448,512... | collective-permute-start | bytes 442376 | tf_op jit(solution)/shard_map/ppermute | solution.py:26
  17.5 6.3 %collective-permute-start.1 = (f32[4,72,128]{2,1,0:T(8,128)S(1)}, f32[4,72,128]{2,1,0:T(8,128)S(1)}, u32[]{:S(2)}, u32[]{:S(2)}) collective-permute-start(f32[4,72,128]{2,1,0:T(8,128)S(1)} %get-tuple-element.24), channel_id=1, source_target_pairs={{0,64},{64,0},{128,192},{192,128},{256,320},{320,256},{384,448},{4... | collective-permute-start | bytes 442376 | tf_op jit(solution)/shard_map/ppermute | solution.py:26
  20.1 3.7 %copy-start.7 = (bf16[64,16]{0,1:T(8,128)(2,1)S(1)}, bf16[64,16]{0,1:T(8,128)(2,1)}, u32[]{:S(2)}) copy-start(bf16[64,16]{0,1:T(8,128)(2,1)} %param.22) | copy-start | bytes 6148
  23.9 9.6 %collective-permute-start.2 = (f32[6,72,128]{2,1,0:T(8,128)S(1)}, f32[6,72,128]{2,1,0:T(8,128)S(1)}, u32[]{:S(2)}, u32[]{:S(2)}) collective-permute-start(f32[6,72,128]{2,1,0:T(8,128)S(1)} %get-tuple-element.27), channel_id=1, source_target_pairs={{1,2},{2,1},{3,4},{4,3},{5,6},{6,5},{7,8},{8,7},{9,10},{10,9},{11,... | collective-permute-start | bytes 663560 | tf_op jit(solution)/shard_map/ppermute | solution.py:26
  28.9 5.7 %collective-permute-start.3 = (f32[6,72,128]{2,1,0:T(8,128)S(1)}, f32[6,72,128]{2,1,0:T(8,128)S(1)}, u32[]{:S(2)}, u32[]{:S(2)}) collective-permute-start(f32[6,72,128]{2,1,0:T(8,128)S(1)} %get-tuple-element.28), channel_id=1, source_target_pairs={{0,1},{1,0},{2,3},{3,2},{4,5},{5,4},{6,7},{7,6},{8,9},{9,8},{10,11... | collective-permute-start | bytes 663560 | tf_op jit(solution)/shard_map/ppermute | solution.py:26
  45.5 5.6 %collective-permute-start.4 = (f32[3,6,128]{2,1,0:T(8,128)S(1)}, f32[3,6,128]{2,1,0:T(8,128)S(1)}, u32[]{:S(2)}, u32[]{:S(2)}) collective-permute-start(f32[3,6,128]{2,1,0:T(8,128)S(1)} %get-tuple-element.37), channel_id=1, source_target_pairs={{64,128},{128,64},{192,256},{256,192},{320,384},{384,320},{448,512... | collective-permute-start | bytes 27656 | tf_op jit(solution)/shard_map/ppermute | solution.py:26
  47.7 4.4 %collective-permute-start.5 = (f32[3,6,128]{2,1,0:T(8,128)S(1)}, f32[3,6,128]{2,1,0:T(8,128)S(1)}, u32[]{:S(2)}, u32[]{:S(2)}) collective-permute-start(f32[3,6,128]{2,1,0:T(8,128)S(1)} %get-tuple-element.38), channel_id=1, source_target_pairs={{0,64},{64,0},{128,192},{192,128},{256,320},{320,256},{384,448},{4... | collective-permute-start | bytes 27656 | tf_op jit(solution)/shard_map/ppermute | solution.py:26
  52.2 6.7 %collective-permute-start.6 = (f32[4,3,128]{2,1,0:T(4,128)S(1)}, f32[4,3,128]{2,1,0:T(4,128)S(1)}, u32[]{:S(2)}, u32[]{:S(2)}) collective-permute-start(f32[4,3,128]{2,1,0:T(4,128)S(1)} %get-tuple-element.40), channel_id=1, source_target_pairs={{0,1},{1,0},{2,3},{3,2},{4,5},{5,4},{6,7},{7,6},{8,9},{9,8},{10,11... | collective-permute-start | bytes 18440 | tf_op jit(solution)/shard_map/ppermute | solution.py:26
  56.9 5.0 %collective-permute-start.7 = (f32[4,3,128]{2,1,0:T(4,128)S(1)}, f32[4,3,128]{2,1,0:T(4,128)S(1)}, u32[]{:S(2)}, u32[]{:S(2)}) collective-permute-start(f32[4,3,128]{2,1,0:T(4,128)S(1)} %get-tuple-element.41), channel_id=1, source_target_pairs={{1,2},{2,1},{3,4},{4,3},{5,6},{6,5},{7,8},{8,7},{9,10},{10,9},{11,... | collective-permute-start | bytes 18440 | tf_op jit(solution)/shard_map/ppermute | solution.py:26
